TPU v7x, 32 devices: a whole 2x2x4 slice. The times are simulated.
32 devices in a mesh: fsdp: 16 (over z, y, core), mp: 2 (over x).
Axes of the slice: x: 2, y: 2, z: 4, core: 2. Of those that a mesh axis runs over, the one named last changes fastest.
Arguments:
- tokens: bfloat16 [8192, 3072], P('fsdp', 'mp'), may hold values from -6 to 6
- ln_gain: float32 [3072], replicated, may hold values from 0.1 to 1.9
- w_qkv: bfloat16 [3072, 3, 3072], P('fsdp', None, 'mp'), may hold values from -0.109375 to 0.109375
- w_up: bfloat16 [3072, 12288], P('fsdp', 'mp'), may hold values from -0.109375 to 0.109375
- q_gain: float32 [24, 128], P('mp'), may hold values from 0.4 to 16
- k_gain: float32 [24, 128], P('mp'), may hold values from 0.4 to 16
- w_proj: bfloat16 [3072, 3072], P('mp', 'fsdp'), may hold values from -0.109375 to 0.109375
- w_down: bfloat16 [12288, 3072], P('mp', 'fsdp'), may hold values from -0.0546875 to 0.0546875
Outputs:
- block_out: bfloat16 [8192, 3072], P('fsdp', 'mp')
All inputs are finite; a program needn't handle non-finite values.
Results may differ from a plain program's by a relative error of at most 0.015.
Values may be sent and summed in bfloat16 or wider, within the bound.
A program may use at most 192 MiB of HBM per device.

v0:
```python
import jax
import jax.numpy as jnp
from jax import lax
from jax.sharding import PartitionSpec as P

HD = 128
PATCHES = 256


def layer_norm(values, gain):
    mean = jnp.mean(values, axis=-1, keepdims=True)
    centred = values - mean
    variance = jnp.mean(centred * centred, axis=-1, keepdims=True)
    return centred * lax.rsqrt(variance + 1e-06) * gain


def local(tokens, ln_gain, w_qkv, w_up, q_gain, k_gain, w_proj, w_down):
    rows = tokens.astype(jnp.float32)
    panels = lax.all_gather(tokens, "mp", axis=1, tiled=True)
    normed = layer_norm(panels.astype(jnp.float32), ln_gain).astype(jnp.bfloat16)
    tok_count = panels.shape[0]
    head_cols = w_qkv.shape[2]
    heads_here = q_gain.shape[0]
    columns = normed
    projected = jnp.einsum(
        "td,dca->cta",
        columns,
        lax.all_gather(w_qkv, "fsdp", axis=0, tiled=True),
        preferred_element_type=jnp.float32,
    )
    columns = normed
    hidden_pre = jnp.dot(
        columns,
        lax.all_gather(w_up, "fsdp", axis=0, tiled=True),
        preferred_element_type=jnp.float32,
    )
    images = tok_count // PATCHES
    queries = layer_norm(projected[0].reshape(tok_count, heads_here, HD), q_gain).astype(
        jnp.bfloat16
    )
    keys = layer_norm(projected[1].reshape(tok_count, heads_here, HD), k_gain).astype(jnp.bfloat16)
    values = projected[2].reshape(tok_count, heads_here, HD).astype(jnp.bfloat16)
    queries = queries.reshape(images, PATCHES, heads_here, HD)
    keys = keys.reshape(images, PATCHES, heads_here, HD)
    values = values.reshape(images, PATCHES, heads_here, HD)
    scores = jnp.einsum(
        "iqhd,ikhd->ihqk", queries, keys, preferred_element_type=jnp.float32
    ) * HD ** (-0.5)
    scores = scores - jnp.max(scores, axis=-1, keepdims=True)
    weights = jnp.exp(scores)
    probs = (weights / jnp.sum(weights, axis=-1, keepdims=True)).astype(jnp.bfloat16)
    attended = jnp.einsum("ihqk,ikhd->iqhd", probs, values, preferred_element_type=jnp.float32)
    attended = attended.astype(jnp.bfloat16).reshape(tok_count, head_cols)
    activated = jax.nn.gelu(hidden_pre, approximate=False).astype(jnp.bfloat16)
    joined = jnp.concatenate([attended, activated], axis=1)
    out_rows = jnp.concatenate([w_proj, w_down], axis=0)
    terms = jnp.dot(
        joined,
        lax.all_gather(out_rows, "fsdp", axis=1, tiled=True),
        preferred_element_type=jnp.float32,
    )
    branches = lax.psum_scatter(
        terms.astype(jnp.bfloat16), "mp", scatter_dimension=1, tiled=True
    ).astype(jnp.float32)
    return (rows + branches).astype(jnp.bfloat16)


def solution(mesh):
    return jax.shard_map(
        local,
        mesh=mesh,
        in_specs=(
            P("fsdp", "mp"),
            P(),
            P("fsdp", None, "mp"),
            P("fsdp", "mp"),
            P("mp", None),
            P("mp", None),
            P("mp", "fsdp"),
            P("mp", "fsdp"),
        ),
        out_specs=P("fsdp", "mp"),
        check_vma=False,
    )
```

profile of v0, /device:TPU:0, one launch (start us, length us, event | category | flops | bytes accessed | tf_op | source)
XLA Modules:
  0.0 709.6 jit_solution(7138560760407008489)
XLA Ops:
  6.5 0.0 copy-start.3
  6.5 0.0 all-gather.5.cloned.1.call-start
  6.5 0.7 all-gather.5.cloned.1.call-update
  7.3 0.0 all-gather.7.cloned.1.call-start
  7.3 0.7 all-gather.7.cloned.1.call-update
  8.0 0.0 all-gather.9.cloned.1.call-start
  8.1 0.7 all-gather.9.cloned.1.call-update
  8.7 0.0 copy-start.6
  8.8 0.0 all-gather.11.cloned.1.call-start
  8.8 0.0 copy-done.3
  8.8 2.8 pad_maximum_fusion
  11.6 0.0 all-gather.11.cloned.1.call-update
  11.6 0.0 reduce-scatter.2.cloned.1.call-start
  11.7 44.9 %all-gather.5.cloned.1.call-done = bf16[512,3072]{1,0:T(8,128)(2,1)} async-done(((bf16[512,1536]{1,0:T(8,128)(2,1)}), bf16[512,3072]{1,0:T(8,128)(2,1)}) %all-gather.5.cloned.1.call-update) | async-done | bytes 3145744 | tf_op jit(solution)/shard_map/all_gather | solution.py:19
  56.6 0.0 copy-start
  56.6 2.5 convert_reduce_fusion
  59.1 2.8 fusion.17
  62.0 139.6 %all-gather.7.cloned.1.call-done = bf16[3072,3,1536]{2,0,1:T(8,128)(2,1)} async-done(((bf16[192,3,1536]{2,0,1:T(8,128)(2,1)}), bf16[3072,3,1536]{2,0,1:T(8,128)(2,1)}) %all-gather.7.cloned.1.call-update) | async-done | bytes 28311568 | tf_op jit(solution)/shard_map/all_gather | solution.py:28
  201.5 0.0 copy-done.6
  201.5 0.0 copy-done
  201.5 19.1 %convolution_bitcast_fusion = f32[3,512,1536]{2,1,0:T(8,128)S(1)} fusion(bf16[3072,3,1536]{2,0,1:T(8,128)(2,1)} %all-gather.7.cloned.1.call-done, bf16[512,3072]{1,0:T(8,128)(2,1)S(1)} %copy-done, f32[3072]{0:T(1024)S(1)} %copy-done.6, f32[512]{0:T(512)S(1)} %add_rsqrt_fusion.2, f32[512]{0:T(512)S(1)} %broadcast_multiply_fusion.2), kind=kOutput, calls=%fused_computation.35 | convolution fusion | flops 14503378944 | bytes 40910848 | tf_op jit(solution)/shard_map/td,dca->cta/dot_general | solution.py:25
  220.6 1.3 slice.17
  221.9 3.0 fusion.44
  225.0 2.6 copy.14
  227.6 3.3 reshape_squeeze.11
  231.0 0.4 reduce_sum.65
  231.4 0.5 multiply_reduce_fusion.2
  231.9 2.4 copy.16
  234.3 3.4 reshape_squeeze.13
  237.7 0.0 copy-start.4
  237.7 0.0 copy-start.5
  237.7 0.4 reduce_sum.67
  238.1 0.5 multiply_reduce_fusion.1
  238.6 2.9 reshape.87
  241.5 0.0 copy-done.4
  241.5 0.0 copy-done.5
  241.6 7.6 %multiply_convert_fusion = (bf16[2,256,12,128]{1,0,3,2:T(2,128)(2,1)S(1)}, bf16[2,256,12,128]{1,0,3,2:T(2,128)(2,1)S(1)}) fusion(f32[2,256,12,128]{1,0,3,2:T(2,128)} %reshape_squeeze.13, f32[12,128]{1,0:T(8,128)S(1)} %copy-done.4, f32[2,256,12]{1,0,2:T(2,128)S(1)} %rsqrt.34, f32[2,256,12]{1,0,2:T(2,128)S(1)} %div.36, f32[12,128]{1,0:T(8,128)S(1)} %copy-done.5, ...), kind=kLoop, calls=%fused_computation.41 | loop fusion | flops 6291456 | bytes 9547776 | tf_op jit(solution)/shard_map/convert_element_type | solution.py:41
  249.2 1.0 fusion.31
  250.2 4.8 fusion.45
  255.0 2.1 fusion.34
  257.1 0.0 copy-start.1
  257.1 4.6 copy.27
  261.7 3.1 copy.39
  264.9 126.1 %all-gather.9.cloned.1.call-done = bf16[3072,6144]{1,0:T(8,128)(2,1)} async-done(((bf16[192,6144]{1,0:T(8,128)(2,1)}), bf16[3072,6144]{1,0:T(8,128)(2,1)}) %all-gather.9.cloned.1.call-update) | async-done | bytes 37748752 | tf_op jit(solution)/shard_map/all_gather | solution.py:34
  391.0 0.0 copy-done.1
  391.0 51.8 %fusion.3 = bf16[512,6144]{1,0:T(8,128)(2,1)} fusion(bf16[3072,6144]{1,0:T(8,128)(2,1)} %all-gather.9.cloned.1.call-done, bf16[512,3072]{1,0:T(8,128)(2,1)S(1)} %copy-done.1, f32[3072]{0:T(1024)S(1)} %copy-done.6, f32[512]{0:T(512)S(1)} %add_rsqrt_fusion.2, f32[512]{0:T(512)S(1)} %broadcast_multiply_fusion.2), kind=kOutput, calls=%fused_computation.4 | convolution fusion | flops 19539689472 | bytes 47202304 | tf_op jit(solution)/shard_map/dot_general | solution.py:32
  442.7 182.0 %all-gather.11.cloned.1.call-done = bf16[7680,3072]{0,1:T(8,128)(2,1)} async-done(((bf16[7680,192]{0,1:T(8,128)(2,1)}), bf16[7680,3072]{0,1:T(8,128)(2,1)}) %all-gather.11.cloned.1.call-update) | async-done | bytes 47185936 | tf_op jit(solution)/shard_map/all_gather | solution.py:59
  624.7 0.0 copy-start.2
  624.7 31.9 %fusion.21 = bf16[512,3072]{1,0:T(8,128)(2,1)} fusion(bf16[7680,3072]{0,1:T(8,128)(2,1)} %all-gather.11.cloned.1.call-done, bf16[512,6144]{1,0:T(8,128)(2,1)} %fusion.3, bf16[512,1536]{1,0:T(8,128)(2,1)} %bitcast.34), kind=kOutput, calls=%fused_computation.36 | convolution fusion | flops 24176492544 | bytes 58195968 | tf_op jit(solution)/shard_map/dot_general | solution.py:57
  656.7 0.0 reduce-scatter.2.cloned.1.call-update
  656.7 43.5 %reduce-scatter.2.cloned.1.call-done = bf16[512,1536]{1,0:T(8,128)(2,1)} async-done(((bf16[512,3072]{1,0:T(8,128)(2,1)}), bf16[512,1536]{1,0:T(8,128)(2,1)}) %reduce-scatter.2.cloned.1.call-update) | async-done | bytes 1572880 | tf_op jit(solution)/shard_map/reduce_scatter | solution.py:62
  700.2 0.0 copy-done.2
  700.2 2.9 add_convert_fusion
  (10 shorter events, 0.1 us)
Async XLA Ops:
  6.5 2.3 copy-start.3
  6.5 50.0 %all-gather.5.cloned.1.call-start = ((), (), s32[]{:S(2)}) async-start(), calls=%async_computation.1 | async-start | bytes 4718592 | tf_op jit(solution)/shard_map/all_gather | solution.py:19
  7.3 194.3 %all-gather.7.cloned.1.call-start = ((), (), s32[]{:S(2)}) async-start(), calls=%async_computation.2 | async-start | bytes 30081024 | tf_op jit(solution)/shard_map/all_gather | solution.py:28
  8.0 383.0 %all-gather.9.cloned.1.call-start = ((), (), s32[]{:S(2)}) async-start(), calls=%async_computation.3 | async-start | bytes 40108032 | tf_op jit(solution)/shard_map/all_gather | solution.py:34
  8.7 192.8 %copy-start.6 = (f32[3072]{0:T(1024)S(1)}, f32[3072]{0:T(1024)}, u32[]{:S(2)}) copy-start(f32[3072]{0:T(1024)} %param.9) | copy-start | bytes 36868
  8.8 616.0 %all-gather.11.cloned.1.call-start = ((), (), s32[]{:S(2)}) async-start(), calls=%async_computation.4 | async-start | bytes 50135040 | tf_op jit(solution)/shard_map/all_gather | solution.py:59
  11.6 688.5 %reduce-scatter.2.cloned.1.call-start = ((), (), s32[]{:S(2)}) async-start(), calls=%async_computation.5 | async-start | bytes 4718592 | tf_op jit(solution)/shard_map/reduce_scatter | solution.py:62
  56.6 145.0 %copy-start = (bf16[512,3072]{1,0:T(8,128)(2,1)S(1)}, bf16[512,3072]{1,0:T(8,128)(2,1)}, u32[]{:S(2)}) copy-start(bf16[512,3072]{1,0:T(8,128)(2,1)} %all-gather.5.cloned.1.call-done) | copy-start | bytes 9437188
  237.7 3.8 copy-start.4
  237.7 3.9 copy-start.5
  257.1 133.8 %copy-start.1 = (bf16[512,3072]{1,0:T(8,128)(2,1)S(1)}, bf16[512,3072]{1,0:T(8,128)(2,1)}, u32[]{:S(2)}) copy-start(bf16[512,3072]{1,0:T(8,128)(2,1)} %all-gather.5.cloned.1.call-done) | copy-start | bytes 9437188
  624.7 75.4 %copy-start.2 = (bf16[512,1536]{1,0:T(8,128)(2,1)S(1)}, bf16[512,1536]{1,0:T(8,128)(2,1)}, u32[]{:S(2)}) copy-start(bf16[512,1536]{1,0:T(8,128)(2,1)} %param.8) | copy-start | bytes 4718596
Sparse Core Ops, SparseCore 0:
  8.9 47.6 all-gather.4
  58.1 143.3 all-gather.6
  203.1 187.7 all-gather.8
  392.4 232.2 all-gather.10
  656.8 43.3 reduce-scatter.1
where the time goes:
time: 710 us
  waiting for transfers between devices  538 us (76%)
  matrix products  106 us (15%)
  local copies, waits for them, and re-layouts  26.9 us (4%)
  other arithmetic  25.2 us (4%)
  between operations  13.3 us (2%)
    all_gather x1, waiting for transfers between devices, local(): lax.all_gather(out_rows, 'fsdp', axis=1, tiled=True)  182 us
    all_gather x1, waiting for transfers between devices, local(): lax.all_gather(w_qkv, 'fsdp', axis=0, tiled=True)  140 us
    all_gather x1, waiting for transfers between devices, local(): lax.all_gather(w_up, 'fsdp', axis=0, tiled=True)  126 us
    dot_general x1, matrix products, local(): jnp.dot(columns, lax.all_gather(w_up, 'fsdp', axis=0, tiled=True), prefer...  51.8 us
    all_gather x1, waiting for transfers between devices, local(): panels = lax.all_gather(tokens, 'mp', axis=1, tiled=True)  44.9 us
    reduce_scatter x1, waiting for transfers between devices, local(): lax.psum_scatter(terms.astype(jnp.bfloat16), 'mp', scatter_dimension=1, t...  43.5 us
    dot_general x1, matrix products, local(): jnp.dot(joined, lax.all_gather(out_rows, 'fsdp', axis=1, tiled=True), pre...  31.9 us
    dot_general x1, matrix products, local(): jnp.einsum('td,dca->cta', columns, lax.all_gather(w_qkv, 'fsdp', axis=0,...  19.1 us
  transfers between devices with their start and end apart: 5, of which 5 were waited for; matrix products, arithmetic and copies ran while one was open for 17% of the time, Pallas kernels for 0%

commit v1 on v0

v1 whole, which is shorter than its diff:
```python
import jax
import jax.numpy as jnp
from jax import lax
from jax.sharding import PartitionSpec as P

HD = 128
PATCHES = 256


def layer_norm(values, gain):
    mean = jnp.mean(values, axis=-1, keepdims=True)
    centred = values - mean
    variance = jnp.mean(centred * centred, axis=-1, keepdims=True)
    return centred * lax.rsqrt(variance + 1e-06) * gain


def attention(projected, q_gain, k_gain):
    tok_count = projected[0].shape[0]
    heads = q_gain.shape[0]
    images = tok_count // PATCHES
    queries = layer_norm(projected[0].reshape(tok_count, heads, HD), q_gain)
    keys = layer_norm(projected[1].reshape(tok_count, heads, HD), k_gain)
    split = (images, PATCHES, heads, HD)
    queries = queries.astype(jnp.bfloat16).reshape(split)
    keys = keys.astype(jnp.bfloat16).reshape(split)
    values = projected[2].astype(jnp.bfloat16).reshape(split)
    scores = jnp.einsum(
        "iqhd,ikhd->ihqk", queries, keys, preferred_element_type=jnp.float32
    ) * HD ** (-0.5)
    scores = scores - jnp.max(scores, axis=-1, keepdims=True)
    weights = jnp.exp(scores)
    probs = (weights / jnp.sum(weights, axis=-1, keepdims=True)).astype(jnp.bfloat16)
    attended = jnp.einsum("ihqk,ikhd->iqhd", probs, values, preferred_element_type=jnp.float32)
    return attended.astype(jnp.bfloat16).reshape(tok_count, heads * HD)


def gathered(tokens, ln_gain, w_qkv, w_up, q_gain, k_gain, w_proj, w_down):
    rows = tokens.astype(jnp.float32)
    panels = lax.all_gather(tokens, "mp", axis=1, tiled=True)
    normed = layer_norm(panels.astype(jnp.float32), ln_gain).astype(jnp.bfloat16)
    projected = jnp.einsum(
        "td,dca->cta",
        normed,
        lax.all_gather(w_qkv, "fsdp", axis=0, tiled=True),
        preferred_element_type=jnp.float32,
    )
    hidden_pre = jnp.dot(
        normed,
        lax.all_gather(w_up, "fsdp", axis=0, tiled=True),
        preferred_element_type=jnp.float32,
    )
    attended = attention(projected, q_gain, k_gain)
    activated = jax.nn.gelu(hidden_pre, approximate=False).astype(jnp.bfloat16)
    joined = jnp.concatenate([attended, activated], axis=1)
    out_rows = jnp.concatenate([w_proj, w_down], axis=0)
    terms = jnp.dot(
        joined,
        lax.all_gather(out_rows, "fsdp", axis=1, tiled=True),
        preferred_element_type=jnp.float32,
    )
    branches = lax.psum_scatter(
        terms.astype(jnp.bfloat16), "mp", scatter_dimension=1, tiled=True
    ).astype(jnp.float32)
    return (rows + branches).astype(jnp.bfloat16)


def paired(n):
    planes = n // 4
    core_bit, y_bit, z_bit = 1, 2, 4

    def swap(value, mask, axis="fsdp"):
        count = n if axis == "fsdp" else 2
        return lax.ppermute(value, axis, [(i, i ^ mask) for i in range(count)])

    def local(tokens, ln_gain, w_qkv, w_up, q_gain, k_gain, w_proj, w_down):
        me = lax.axis_index("fsdp")
        side = lax.axis_index("mp")
        half = (me // z_bit) % 2
        tok_count = tokens.shape[0]
        depth = w_up.shape[0]
        heads = q_gain.shape[0] // 2
        head_cols, hidden = heads * HD, w_up.shape[1] // 2

        def in_half(which):
            qkv = lax.dynamic_slice_in_dim(w_qkv, which * head_cols, head_cols, 2)
            up = lax.dynamic_slice_in_dim(w_up, which * hidden, hidden, 1)
            return jnp.concatenate([qkv.reshape(depth, 3 * head_cols), up], axis=1)

        def out_half(which):
            proj = lax.dynamic_slice_in_dim(w_proj, which * head_cols, head_cols, 0)
            down = lax.dynamic_slice_in_dim(w_down, which * hidden, hidden, 0)
            return jnp.concatenate([proj, down], axis=0).T

        def spread(make_half, after):
            mine, other = make_half(half), make_half(1 - half)
            if after:
                mine, other, _ = lax.optimization_barrier((mine, other, after))
            blocks = []
            for k in range(planes):
                here = mine if k == 0 else swap(other if k % 2 else mine, k * z_bit)
                across = swap(here, y_bit)
                blocks.append([here, swap(here, core_bit), across, swap(across, core_bit)])
            return blocks

        both = jnp.concatenate([tokens, swap(tokens, z_bit)], axis=0)
        peer = swap(both, 1, "mp")
        first = jnp.where(side == 0, both, peer)
        second = jnp.where(side == 0, peer, both)
        panels = jnp.concatenate([first, second], axis=1)
        normed = layer_norm(panels.astype(jnp.float32), ln_gain).astype(jnp.bfloat16)

        in_blocks = spread(in_half, ())
        out_blocks = spread(out_half, [blocks[0] for blocks in in_blocks[1:]])

        w_in = jnp.zeros((n, depth, 3 * head_cols + hidden), jnp.bfloat16)
        for k in range(planes):
            for j in range(4):
                w_in = lax.dynamic_update_slice_in_dim(
                    w_in, in_blocks[k][j][None], me ^ (k * z_bit + j), 0
                )
        w_in = w_in.reshape(n * depth, 3 * head_cols + hidden)
        projected = [
            jnp.dot(
                normed,
                w_in[:, c * head_cols : (c + 1) * head_cols],
                preferred_element_type=jnp.float32,
            )
            for c in range(3)
        ]
        gain_q = lax.dynamic_slice_in_dim(q_gain, half * heads, heads, 0)
        gain_k = lax.dynamic_slice_in_dim(k_gain, half * heads, heads, 0)
        attended = attention(projected, gain_q, gain_k)
        hidden_pre = jnp.dot(
            normed, w_in[:, 3 * head_cols :], preferred_element_type=jnp.float32
        )
        activated = jax.nn.gelu(hidden_pre, approximate=False).astype(jnp.bfloat16)
        joined = jnp.concatenate([attended, activated], axis=1)

        def term(k):
            w_out = jnp.zeros((4, depth, joined.shape[1]), jnp.bfloat16)
            for j in range(4):
                w_out = lax.dynamic_update_slice_in_dim(
                    w_out, out_blocks[k][j][None], (me % 4) ^ j, 0
                )
            return lax.dot_general(
                joined,
                w_out.reshape(4 * depth, joined.shape[1]),
                (((1,), (1,)), ((), ())),
                preferred_element_type=jnp.float32,
            ).astype(jnp.bfloat16)

        keep_low = (me // (2 * z_bit)) % 2 == side
        own, far = [], []
        for stage in range(2):
            low, high = term(stage), term(stage + 2)
            keep = jnp.where(keep_low, low, high)
            got = swap(jnp.where(keep_low, high, low), 1, "mp")
            total = keep.astype(jnp.float32) + got.astype(jnp.float32)
            own.append(total[:tok_count])
            far.append(swap(total[tok_count:].astype(jnp.bfloat16), z_bit))
        done = [own[s] + far[1 - s].astype(jnp.float32) for s in range(2)]
        branches = jnp.where(
            half == 0,
            jnp.concatenate(done, axis=1),
            jnp.concatenate(done[::-1], axis=1),
        )
        return (tokens.astype(jnp.float32) + branches).astype(jnp.bfloat16)

    return local


def solution(mesh):
    n, sides = mesh.shape["fsdp"], mesh.shape["mp"]
    return jax.shard_map(
        paired(n) if (n, sides) == (16, 2) else gathered,
        mesh=mesh,
        in_specs=(
            P("fsdp", "mp"),
            P(),
            P("fsdp", None, "mp"),
            P("fsdp", "mp"),
            P("mp", None),
            P("mp", None),
            P("mp", "fsdp"),
            P("mp", "fsdp"),
        ),
        out_specs=P("fsdp", "mp"),
        check_vma=False,
    )
```

time: 710 us -> 839 us (1.18); the launches traced: 710 us -> 830 us
  local copies, waits for them, and re-layouts: 26.9 us -> 114 us
  starting transfers between devices: 0.16 us -> 24.6 us
  matrix products: 106 us -> 121 us
  between operations: 13.3 us -> 1.16 us
  other arithmetic: 25.2 us -> 34.8 us
    ppermute x0 -> x36, waiting for transfers between devices: none -> 534 us  [swap(): return lax.ppermute(value, axis, [(i, i ^ mask) for i in range(count)])]
    all_gather x4 -> x0, waiting for transfers between devices: 493 us -> none  [the longest x1 182 us: local(): lax.all_gather(out_rows, 'fsdp', axis=1, tiled=True)]
    dynamic_update_slice x0 -> x31, local copies, waits for them, and re-layouts: none -> 54.5 us  [the longest x15 30.1 us: local(): lax.dynamic_update_slice_in_dim(w_in, in_blocks[k][j][None], me ^ k * z_b...]
    reduce_scatter x1 -> x0, waiting for transfers between devices: 43.5 us -> none  [local(): lax.psum_scatter(terms.astype(jnp.bfloat16), 'mp', scatter_dimension=1, t...]
    ppermute x0 -> x36, starting transfers between devices: none -> 24.6 us  [swap(): return lax.ppermute(value, axis, [(i, i ^ mask) for i in range(count)])]
    reshape x1 -> x8, local copies, waits for them, and re-layouts: 4.6 us -> 23.7 us  [the longest x2 10.1 us: attention(): queries = layer_norm(projected[0].reshape(tok_count, heads, HD), q_gain)]
    dot_general x5 -> x10, matrix products: 106 us -> 121 us  [the longest x1 55 us: local(): jnp.dot(normed, w_in[:, 3 * head_cols:], preferred_element_type=jnp.float32)]
    broadcast_in_dim x0 -> x1, local copies, waits for them, and re-layouts: none -> 10.7 us  [local(): w_in = jnp.zeros((n, depth, 3 * head_cols + hidden), jnp.bfloat16)]
  transfers between devices with their start and end apart: 5 -> 36, of which waited for: 5 -> 11; matrix products, arithmetic and copies ran while one was open for 17% -> 31% of each run, Pallas kernels for 0% -> 0%
where the time goes in v1:
time: 839 us; the launch traced here: 830 us
  waiting for transfers between devices  534 us (64%)
  matrix products  121 us (14%)
  local copies, waits for them, and re-layouts  114 us (14%)
  other arithmetic  34.8 us (4%)
  starting transfers between devices  24.6 us (3%)
    ppermute x36, waiting for transfers between devices, swap(): return lax.ppermute(value, axis, [(i, i ^ mask) for i in range(count)])  534 us
    dot_general x1, matrix products, local(): jnp.dot(normed, w_in[:, 3 * head_cols:], preferred_element_type=jnp.float32)  55 us
    dot_general x4, matrix products, term(): lax.dot_general(joined, w_out.reshape(4 * depth, joined.shape[1]), (((1,)...  32.6 us
    dynamic_update_slice x15, local copies, waits for them, and re-layouts, local(): lax.dynamic_update_slice_in_dim(w_in, in_blocks[k][j][None], me ^ k * z_b...  30.1 us
    ppermute x36, starting transfers between devices, swap(): return lax.ppermute(value, axis, [(i, i ^ mask) for i in range(count)])  24.6 us
    dynamic_update_slice x16, local copies, waits for them, and re-layouts, term(): lax.dynamic_update_slice_in_dim(w_out, out_blocks[k][j][None], me % 4 ^ j...  24.4 us
    dot_general x3, matrix products, local(): jnp.dot(normed, w_in[:, c * head_cols:(c + 1) * head_cols], preferred_ele...  24 us
  transfers between devices with their start and end apart: 36, of which 11 were waited for; matrix products, arithmetic and copies ran while one was open for 31% of the time, Pallas kernels for 0%

profile of v1, /device:TPU:0, one launch (start us, length us, event | category | flops | bytes accessed | tf_op | source)
XLA Modules:
  0.0 829.8 jit_solution(15730852219096661646)
XLA Ops:
  0.0 1.5 dynamic-slice_bitcast_fusion.1
  1.6 1.8 constant_dynamic-slice_fusion.7
  5.3 3.6 collective-permute-start.9
  10.5 1.6 collective-permute-start.5
  12.9 1.6 constant_dynamic-slice_fusion
  14.6 2.9 maximum_bitcast_fusion
  17.5 10.7 %broadcast_in_dim.110 = bf16[16,192,5376]{2,1,0:T(8,128)(2,1)} broadcast(bf16[]{:T(256)} %constant.151.clone.1), dimensions={} | broadcast | bytes 33030146 | tf_op jit(solution)/shard_map/broadcast_in_dim | solution.py:115
  29.7 149.1 %collective-permute-done = bf16[512,1536]{1,0:T(8,128)(2,1)} collective-permute-done((bf16[512,1536]{1,0:T(8,128)(2,1)}, bf16[512,1536]{1,0:T(8,128)(2,1)}, u32[]{:S(2)}, u32[]{:S(2)}) %collective-permute-start) | collective-permute-done | bytes 1572896 | tf_op jit(solution)/shard_map/ppermute | solution.py:73
  178.9 1.6 collective-permute-start.3
  184.1 1.6 collective-permute-start.1
  186.2 5.6 collective-permute-start.20
  191.8 3.1 bitcast_dynamic-update-slice_fusion.14
  194.9 32.2 %collective-permute-done.3 = bf16[192,5376]{1,0:T(8,128)(2,1)} collective-permute-done((bf16[192,5376]{1,0:T(8,128)(2,1)}, bf16[192,5376]{1,0:T(8,128)(2,1)}, u32[]{:S(2)}, u32[]{:S(2)}) %collective-permute-start.3) | collective-permute-done | bytes 2064416 | tf_op jit(solution)/shard_map/ppermute | solution.py:73
  227.0 3.1 bitcast_dynamic-update-slice_fusion.13
  230.1 2.9 broadcast.96.clone.2
  234.3 21.9 %collective-permute-done.20 = bf16[192,3840]{1,0:T(8,128)(2,1)} collective-permute-done((bf16[192,3840]{1,0:T(8,128)(2,1)S(1)}, bf16[192,3840]{1,0:T(8,128)(2,1)}, u32[]{:S(2)}, u32[]{:S(2)}) %collective-permute-start.20) | collective-permute-done | bytes 1474592 | tf_op jit(solution)/shard_map/ppermute | solution.py:73
  258.6 60.6 %collective-permute-done.25 = bf16[192,3840]{1,0:T(8,128)(2,1)S(1)} collective-permute-done((bf16[192,3840]{1,0:T(8,128)(2,1)}, bf16[192,3840]{1,0:T(8,128)(2,1)S(1)}, u32[]{:S(2)}, u32[]{:S(2)}) %collective-permute-start.25) | collective-permute-done | bytes 1474592 | tf_op jit(solution)/shard_map/ppermute | solution.py:73
  320.4 2.4 copy-done.4
  326.7 2.6 bitcast_dynamic-update-slice_fusion.29
  331.4 3.0 bitcast_dynamic-update-slice_fusion.11
  334.5 1.5 bitcast_dynamic-update-slice_fusion.10
  336.0 35.4 %collective-permute-done.7 = bf16[192,5376]{1,0:T(8,128)(2,1)S(1)} collective-permute-done((bf16[192,5376]{1,0:T(8,128)(2,1)}, bf16[192,5376]{1,0:T(8,128)(2,1)S(1)}, u32[]{:S(2)}, u32[]{:S(2)}) %collective-permute-start.7) | collective-permute-done | bytes 2064416 | tf_op jit(solution)/shard_map/ppermute | solution.py:73
  372.9 1.7 copy-done.5
  375.1 2.7 broadcast_select_fusion.1
  378.7 3.6 fusion.5
  382.4 4.0 fusion.7
  386.7 2.8 bitcast_dynamic-update-slice_fusion.26
  389.5 101.7 %collective-permute-done.22 = bf16[192,3840]{1,0:T(8,128)(2,1)} collective-permute-done((bf16[192,3840]{1,0:T(8,128)(2,1)}, bf16[192,3840]{1,0:T(8,128)(2,1)}, u32[]{:S(2)}, u32[]{:S(2)}) %collective-permute-start.22) | collective-permute-done | bytes 1474592 | tf_op jit(solution)/shard_map/ppermute | solution.py:73
  491.7 2.6 bitcast_dynamic-update-slice_fusion.25
  495.5 29.7 %collective-permute-done.27 = bf16[192,3840]{1,0:T(8,128)(2,1)} collective-permute-done((bf16[192,3840]{1,0:T(8,128)(2,1)S(1)}, bf16[192,3840]{1,0:T(8,128)(2,1)}, u32[]{:S(2)}, u32[]{:S(2)}) %collective-permute-start.27) | collective-permute-done | bytes 1474592 | tf_op jit(solution)/shard_map/ppermute | solution.py:73
  525.7 2.6 bitcast_dynamic-update-slice_fusion.21
  528.5 29.8 %collective-permute-done.31 = bf16[192,3840]{1,0:T(8,128)(2,1)} collective-permute-done((bf16[192,3840]{1,0:T(8,128)(2,1)S(1)}, bf16[192,3840]{1,0:T(8,128)(2,1)}, u32[]{:S(2)}, u32[]{:S(2)}) %collective-permute-start.31) | collective-permute-done | bytes 1474592 | tf_op jit(solution)/shard_map/ppermute | solution.py:73
  561.0 1.7 bitcast_dynamic-update-slice_fusion.28
  564.1 3.1 bitcast_dynamic-update-slice_fusion.7
  572.2 3.1 bitcast_dynamic-update-slice_fusion.3
  579.7 8.6 %fusion.32 = bf16[1024,768]{1,0:T(8,128)(2,1)} fusion(bf16[1024,3072]{1,0:T(8,128)(2,1)S(1)} %fusion.7, bf16[3072,5376]{1,0:T(8,128)(2,1)} %bitcast.104), kind=kOutput, calls=%fused_computation.77 | convolution fusion | flops 4832624640 | bytes 12582912 | tf_op jit(solution)/shard_map/dot_general | solution.py:123
  588.2 8.3 %fusion.21 = f32[1024,768]{0,1:T(8,128)} fusion(bf16[1024,3072]{1,0:T(8,128)(2,1)S(1)} %fusion.7, bf16[3072,5376]{1,0:T(8,128)(2,1)} %bitcast.105), kind=kOutput, calls=%fused_computation.37 | convolution fusion | flops 4831838208 | bytes 14155776 | tf_op jit(solution)/shard_map/dot_general | solution.py:123
  596.5 7.2 fusion.19
  603.7 55.0 %fusion.10 = bf16[1024,3072]{1,0:T(8,128)(2,1)} fusion(bf16[1024,3072]{1,0:T(8,128)(2,1)S(1)} %fusion.7, bf16[3072,5376]{1,0:T(8,128)(2,1)} %bitcast.107), kind=kOutput, calls=%fused_computation.13 | convolution fusion | flops 19531825152 | bytes 31457280 | tf_op jit(solution)/shard_map/dot_general | solution.py:133
  658.8 4.3 reshape.121
  663.1 5.1 reshape.112
  668.2 2.2 reduce_sum.65
  670.4 2.3 multiply_reduce_fusion.2
  672.8 3.0 reshape.114
  676.6 3.1 copy.22
  679.7 4.9 copy.21
  684.6 7.2 fusion.35
  691.8 4.8 fusion.47
  696.6 2.0 fusion.43
  698.6 3.0 copy.31
  702.0 10.6 %convolution_convert_fusion.3 = bf16[1024,768]{0,1:T(8,128)(2,1)S(1)} fusion(bf16[768,3840]{1,0:T(8,128)(2,1)} %bitcast.30, bf16[1024,3072]{1,0:T(8,128)(2,1)} %fusion.10, bf16[1024,768]{1,0:T(8,128)(2,1)S(1)} %bitcast.125), kind=kOutput, calls=%fused_computation.75 | convolution fusion | flops 6056312832 | bytes 15335424 | tf_op jit(solution)/shard_map/dot_general | solution.py:145
  712.7 1.7 bitcast_dynamic-update-slice_fusion.20
  714.4 6.3 convolution_convert_fusion.1
  720.7 1.7 bitcast_dynamic-update-slice_fusion.16
  722.4 9.4 %broadcast_select_fusion.2 = (bf16[1024,768]{0,1:T(8,128)(2,1)S(1)}, bf16[1024,768]{0,1:T(8,128)(2,1)S(1)}) fusion(bf16[1024,768]{0,1:T(8,128)(2,1)S(1)} %convolution_convert_fusion.1, pred[]{:T(512)S(6)} %eq.30, bf16[768,3840]{1,0:T(8,128)(2,1)S(1)} %bitcast.117, bf16[1024,3072]{1,0:T(8,128)(2,1)} %fusion.10, bf16[1024,768]{1,0:T(8,128)(2,1)S(1)} %bitcast.127), kind=kOutput, calls=%fused_computation.91 | convolution fusion | flops 6057099264 | bytes 18481152 | tf_op jit(solution)/shard_map/dot_general | solution.py:145
  731.8 1.6 collective-permute-start.33
  735.0 6.3 broadcast_select_fusion.3
  741.9 27.3 %collective-permute-done.33 = bf16[1024,768]{0,1:T(8,128)(2,1)S(1)} collective-permute-done((bf16[1024,768]{0,1:T(8,128)(2,1)S(1)}, bf16[1024,768]{0,1:T(8,128)(2,1)S(1)}, u32[]{:S(2)}, u32[]{:S(2)}) %collective-permute-start.33) | collective-permute-done | bytes 1572896 | tf_op jit(solution)/shard_map/ppermute | solution.py:73
  771.1 31.3 %collective-permute-done.24 = bf16[1024,768]{0,1:T(8,128)(2,1)S(1)} collective-permute-done((bf16[1024,768]{0,1:T(8,128)(2,1)S(1)}, bf16[1024,768]{0,1:T(8,128)(2,1)S(1)}, u32[]{:S(2)}, u32[]{:S(2)}) %collective-permute-start.24) | collective-permute-done | bytes 1572896 | tf_op jit(solution)/shard_map/ppermute | solution.py:73
  803.4 1.6 copy-done
  806.0 2.6 copy.17
  808.6 2.0 slice_add_fusion.1
  810.5 14.9 %collective-permute-done.35 = bf16[512,768]{0,1:T(8,128)(2,1)} collective-permute-done((bf16[512,768]{0,1:T(8,128)(2,1)}, bf16[512,768]{0,1:T(8,128)(2,1)}, u32[]{:S(2)}, u32[]{:S(2)}) %collective-permute-start.35) | collective-permute-done | bytes 786464 | tf_op jit(solution)/shard_map/ppermute | solution.py:73
  827.8 1.6 copy.27
  (163 shorter events, 49.6 us)
Async XLA Ops:
  3.4 9.5 %copy-start.6 = (bf16[6144,192]{0,1:T(8,128)(2,1)S(1)}, bf16[6144,192]{0,1:T(8,128)(2,1)}, u32[]{:S(2)}) copy-start(bf16[6144,192]{0,1:T(8,128)(2,1)} %param.15) | copy-start | bytes 7077892
  4.9 9.7 %copy-start.14 = (bf16[1536,192]{0,1:T(8,128)(2,1)S(1)}, bf16[1536,192]{0,1:T(8,128)(2,1)}, u32[]{:S(2)}) copy-start(bf16[1536,192]{0,1:T(8,128)(2,1)} %param.14) | copy-start | bytes 1769476
  4.9 181.4 %collective-permute-start.2 = (bf16[192,5376]{1,0:T(8,128)(2,1)}, bf16[192,5376]{1,0:T(8,128)(2,1)}, u32[]{:S(2)}, u32[]{:S(2)}) collective-permute-start(bf16[192,5376]{1,0:T(8,128)(2,1)} %pad_maximum_fusion.2), channel_id=1, source_target_pairs={{0,2},{2,0},{4,6},{6,4},{8,10},{10,8},{12,14},{14,12},{16,18},{18,... | collective-permute-start | bytes 6193160 | tf_op jit(solution)/shard_map/ppermute | solution.py:73
  5.3 180.3 %collective-permute-start.9 = (bf16[192,5376]{1,0:T(8,128)(2,1)}, bf16[192,5376]{1,0:T(8,128)(2,1)}, u32[]{:S(2)}, u32[]{:S(2)}) collective-permute-start(bf16[192,5376]{1,0:T(8,128)(2,1)} %pad_maximum_fusion.2), channel_id=1, source_target_pairs={{0,16},{2,18},{4,20},{6,22},{8,24},{10,26},{12,28},{14,30},{16,0},... | collective-permute-start | bytes 6193160 | tf_op jit(solution)/shard_map/ppermute | solution.py:73
  10.5 173.6 %collective-permute-start.5 = (bf16[192,5376]{1,0:T(8,128)(2,1)}, bf16[192,5376]{1,0:T(8,128)(2,1)}, u32[]{:S(2)}, u32[]{:S(2)}) collective-permute-start(bf16[192,5376]{1,0:T(8,128)(2,1)} %pad_maximum_fusion.3), channel_id=1, source_target_pairs={{0,8},{2,10},{4,12},{6,14},{8,0},{10,2},{12,4},{14,6},{16,24},{18,... | collective-permute-start | bytes 6193160 | tf_op jit(solution)/shard_map/ppermute | solution.py:73
  12.0 173.6 %collective-permute-start.13 = (bf16[192,5376]{1,0:T(8,128)(2,1)}, bf16[192,5376]{1,0:T(8,128)(2,1)}, u32[]{:S(2)}, u32[]{:S(2)}) collective-permute-start(bf16[192,5376]{1,0:T(8,128)(2,1)} %pad_maximum_fusion.3), channel_id=1, source_target_pairs={{0,24},{2,26},{4,28},{6,30},{8,16},{10,18},{12,20},{14,22},{16,8},... | collective-permute-start | bytes 6193160 | tf_op jit(solution)/shard_map/ppermute | solution.py:73
  12.0 166.8 %collective-permute-start = (bf16[512,1536]{1,0:T(8,128)(2,1)}, bf16[512,1536]{1,0:T(8,128)(2,1)}, u32[]{:S(2)}, u32[]{:S(2)}) collective-permute-start(bf16[512,1536]{1,0:T(8,128)(2,1)} %param.8), channel_id=1, source_target_pairs={{0,8},{2,10},{4,12},{6,14},{8,0},{10,2},{12,4},{14,6},{16,24},{18,... | collective-permute-start | bytes 4718600 | tf_op jit(solution)/shard_map/ppermute | solution.py:73
  17.5 162.9 %copy-start.18 = (f32[12,128]{1,0:T(8,128)S(1)}, f32[12,128]{1,0:T(8,128)}, u32[]{:S(2)}) copy-start(f32[12,128]{1,0:T(8,128)} %param.13) | copy-start | bytes 18436
  17.5 162.9 %copy-start.19 = (f32[12,128]{1,0:T(8,128)S(1)}, f32[12,128]{1,0:T(8,128)}, u32[]{:S(2)}) copy-start(f32[12,128]{1,0:T(8,128)} %param.12) | copy-start | bytes 18436
  178.9 48.2 %collective-permute-start.3 = (bf16[192,5376]{1,0:T(8,128)(2,1)}, bf16[192,5376]{1,0:T(8,128)(2,1)}, u32[]{:S(2)}, u32[]{:S(2)}) collective-permute-start(bf16[192,5376]{1,0:T(8,128)(2,1)} %pad_maximum_fusion.2), channel_id=1, source_target_pairs={{0,4},{2,6},{4,0},{6,2},{8,12},{10,14},{12,8},{14,10},{16,20},{18,... | collective-permute-start | bytes 6193160 | tf_op jit(solution)/shard_map/ppermute | solution.py:73
  184.1 188.9 %collective-permute-start.1 = (bf16[1024,1536]{1,0:T(8,128)(2,1)S(1)}, bf16[1024,1536]{1,0:T(8,128)(2,1)S(1)}, u32[]{:S(2)}, u32[]{:S(2)}) collective-permute-start(bf16[1024,1536]{1,0:T(8,128)(2,1)S(1)} %constant_dynamic-update-slice_fusion), channel_id=1, source_target_pairs={{0,1},{1,0},{2,3},{3,2},{4,5},{5,4},{6,7},{7,6},{8,9},{9,8},{10,11... | collective-permute-start | bytes 9437192 | tf_op jit(solution)/shard_map/ppermute | solution.py:73
  185.6 137.8 %collective-permute-start.17 = (bf16[192,3840]{1,0:T(8,128)(2,1)S(1)}, bf16[192,3840]{1,0:T(8,128)(2,1)S(1)}, u32[]{:S(2)}, u32[]{:S(2)}) collective-permute-start(bf16[192,3840]{1,0:T(8,128)(2,1)S(1)} %get-tuple-element.7), channel_id=1, source_target_pairs={{0,2},{2,0},{4,6},{6,4},{8,10},{10,8},{12,14},{14,12},{16,18},{18,... | collective-permute-start | bytes 4423688 | tf_op jit(solution)/shard_map/ppermute | solution.py:73
  185.6 139.6 %collective-permute-start.18 = (bf16[192,3840]{1,0:T(8,128)(2,1)S(1)}, bf16[192,3840]{1,0:T(8,128)(2,1)}, u32[]{:S(2)}, u32[]{:S(2)}) collective-permute-start(bf16[192,3840]{1,0:T(8,128)(2,1)S(1)} %get-tuple-element.7), channel_id=1, source_target_pairs={{0,4},{2,6},{4,0},{6,2},{8,12},{10,14},{12,8},{14,10},{16,20},{18,... | collective-permute-start | bytes 4423688 | tf_op jit(solution)/shard_map/ppermute | solution.py:73
  186.2 70.0 %collective-permute-start.20 = (bf16[192,3840]{1,0:T(8,128)(2,1)S(1)}, bf16[192,3840]{1,0:T(8,128)(2,1)}, u32[]{:S(2)}, u32[]{:S(2)}) collective-permute-start(bf16[192,3840]{1,0:T(8,128)(2,1)S(1)} %get-tuple-element.7), channel_id=1, source_target_pairs={{0,16},{2,18},{4,20},{6,22},{8,24},{10,26},{12,28},{14,30},{16,0},... | collective-permute-start | bytes 4423688 | tf_op jit(solution)/shard_map/ppermute | solution.py:73
  227.0 92.2 %collective-permute-start.25 = (bf16[192,3840]{1,0:T(8,128)(2,1)}, bf16[192,3840]{1,0:T(8,128)(2,1)S(1)}, u32[]{:S(2)}, u32[]{:S(2)}) collective-permute-start(bf16[192,3840]{1,0:T(8,128)(2,1)} %get-tuple-element.8), channel_id=1, source_target_pairs={{0,8},{2,10},{4,12},{6,14},{8,0},{10,2},{12,4},{14,6},{16,24},{18,... | collective-permute-start | bytes 4423688 | tf_op jit(solution)/shard_map/ppermute | solution.py:73
  256.2 64.1 %collective-permute-start.29 = (bf16[192,3840]{1,0:T(8,128)(2,1)}, bf16[192,3840]{1,0:T(8,128)(2,1)S(1)}, u32[]{:S(2)}, u32[]{:S(2)}) collective-permute-start(bf16[192,3840]{1,0:T(8,128)(2,1)} %get-tuple-element.8), channel_id=1, source_target_pairs={{0,24},{2,26},{4,28},{6,30},{8,16},{10,18},{12,20},{14,22},{16,8},... | collective-permute-start | bytes 4423688 | tf_op jit(solution)/shard_map/ppermute | solution.py:73
  258.6 61.8 %copy-start.3 = (bf16[4,192,3840]{2,1,0:T(8,128)(2,1)}, bf16[4,192,3840]{2,1,0:T(8,128)(2,1)S(1)}, u32[]{:S(2)}) copy-start(bf16[4,192,3840]{2,1,0:T(8,128)(2,1)S(1)} %bitcast_dynamic-update-slice_fusion.27) | copy-start | bytes 17694724
  319.2 10.1 %collective-permute-start.4 = (bf16[192,5376]{1,0:T(8,128)(2,1)}, bf16[192,5376]{1,0:T(8,128)(2,1)S(1)}, u32[]{:S(2)}, u32[]{:S(2)}) collective-permute-start(bf16[192,5376]{1,0:T(8,128)(2,1)} %collective-permute-done.3), channel_id=1, source_target_pairs={{0,2},{2,0},{4,6},{6,4},{8,10},{10,8},{12,14},{14,12},{16,18},{18,... | collective-permute-start | bytes 6193160 | tf_op jit(solution)/shard_map/ppermute | solution.py:73
  320.4 2.5 copy-start.4
  322.8 2.4 copy-start.10
  322.8 11.6 %collective-permute-start.6 = (bf16[192,5376]{1,0:T(8,128)(2,1)}, bf16[192,5376]{1,0:T(8,128)(2,1)S(1)}, u32[]{:S(2)}, u32[]{:S(2)}) collective-permute-start(bf16[192,5376]{1,0:T(8,128)(2,1)} %collective-permute-done.5), channel_id=1, source_target_pairs={{0,2},{2,0},{4,6},{6,4},{8,10},{10,8},{12,14},{14,12},{16,18},{18,... | collective-permute-start | bytes 6193160 | tf_op jit(solution)/shard_map/ppermute | solution.py:73
  323.4 48.0 %collective-permute-start.7 = (bf16[192,5376]{1,0:T(8,128)(2,1)}, bf16[192,5376]{1,0:T(8,128)(2,1)S(1)}, u32[]{:S(2)}, u32[]{:S(2)}) collective-permute-start(bf16[192,5376]{1,0:T(8,128)(2,1)} %collective-permute-done.5), channel_id=1, source_target_pairs={{0,4},{2,6},{4,0},{6,2},{8,12},{10,14},{12,8},{14,10},{16,20},{18,... | collective-permute-start | bytes 6193160 | tf_op jit(solution)/shard_map/ppermute | solution.py:73
  325.2 234.6 %collective-permute-start.11 = (bf16[192,5376]{1,0:T(8,128)(2,1)}, bf16[192,5376]{1,0:T(8,128)(2,1)S(1)}, u32[]{:S(2)}, u32[]{:S(2)}) collective-permute-start(bf16[192,5376]{1,0:T(8,128)(2,1)} %collective-permute-done.9), channel_id=1, source_target_pairs={{0,4},{2,6},{4,0},{6,2},{8,12},{10,14},{12,8},{14,10},{16,20},{18,... | collective-permute-start | bytes 6193160 | tf_op jit(solution)/shard_map/ppermute | solution.py:73
  329.3 231.2 %collective-permute-start.15 = (bf16[192,5376]{1,0:T(8,128)(2,1)}, bf16[192,5376]{1,0:T(8,128)(2,1)S(1)}, u32[]{:S(2)}, u32[]{:S(2)}) collective-permute-start(bf16[192,5376]{1,0:T(8,128)(2,1)} %collective-permute-done.13), channel_id=1, source_target_pairs={{0,4},{2,6},{4,0},{6,2},{8,12},{10,14},{12,8},{14,10},{16,20},{18,... | collective-permute-start | bytes 6193160 | tf_op jit(solution)/shard_map/ppermute | solution.py:73
  334.5 226.1 %collective-permute-start.19 = (bf16[192,3840]{1,0:T(8,128)(2,1)}, bf16[192,3840]{1,0:T(8,128)(2,1)S(1)}, u32[]{:S(2)}, u32[]{:S(2)}) collective-permute-start(bf16[192,3840]{1,0:T(8,128)(2,1)} %collective-permute-done.18), channel_id=1, source_target_pairs={{0,2},{2,0},{4,6},{6,4},{8,10},{10,8},{12,14},{14,12},{16,18},{18,... | collective-permute-start | bytes 4423688 | tf_op jit(solution)/shard_map/ppermute | solution.py:73
  371.4 6.4 copy-start.8
  371.4 15.0 %collective-permute-start.21 = (bf16[192,3840]{1,0:T(8,128)(2,1)}, bf16[192,3840]{1,0:T(8,128)(2,1)}, u32[]{:S(2)}, u32[]{:S(2)}) collective-permute-start(bf16[192,3840]{1,0:T(8,128)(2,1)} %collective-permute-done.20), channel_id=1, source_target_pairs={{0,2},{2,0},{4,6},{6,4},{8,10},{10,8},{12,14},{14,12},{16,18},{18,... | collective-permute-start | bytes 4423688 | tf_op jit(solution)/shard_map/ppermute | solution.py:73
  372.9 1.7 copy-start.5
  374.6 116.6 %collective-permute-start.22 = (bf16[192,3840]{1,0:T(8,128)(2,1)}, bf16[192,3840]{1,0:T(8,128)(2,1)}, u32[]{:S(2)}, u32[]{:S(2)}) collective-permute-start(bf16[192,3840]{1,0:T(8,128)(2,1)} %collective-permute-done.20), channel_id=1, source_target_pairs={{0,4},{2,6},{4,0},{6,2},{8,12},{10,14},{12,8},{14,10},{16,20},{18,... | collective-permute-start | bytes 4423688 | tf_op jit(solution)/shard_map/ppermute | solution.py:73
  377.8 4.5 copy-start.17
  382.4 4.0 copy-start.13
  386.3 108.0 %copy-start.11 = (bf16[192,3840]{1,0:T(8,128)(2,1)S(1)}, bf16[192,3840]{1,0:T(8,128)(2,1)}, u32[]{:S(2)}) copy-start(bf16[192,3840]{1,0:T(8,128)(2,1)} %copy-done.10) | copy-start | bytes 4423684
  386.4 142.0 %copy-start.9 = (bf16[192,5376]{1,0:T(8,128)(2,1)S(1)}, bf16[192,5376]{1,0:T(8,128)(2,1)}, u32[]{:S(2)}) copy-start(bf16[192,5376]{1,0:T(8,128)(2,1)} %copy-done.8) | copy-start | bytes 6193156
  386.4 107.9 %collective-permute-start.26 = (bf16[192,3840]{1,0:T(8,128)(2,1)S(1)}, bf16[192,3840]{1,0:T(8,128)(2,1)S(1)}, u32[]{:S(2)}, u32[]{:S(2)}) collective-permute-start(bf16[192,3840]{1,0:T(8,128)(2,1)S(1)} %copy-done.13), channel_id=1, source_target_pairs={{0,2},{2,0},{4,6},{6,4},{8,10},{10,8},{12,14},{14,12},{16,18},{18,... | collective-permute-start | bytes 4423688 | tf_op jit(solution)/shard_map/ppermute | solution.py:73
  491.2 34.0 %collective-permute-start.27 = (bf16[192,3840]{1,0:T(8,128)(2,1)S(1)}, bf16[192,3840]{1,0:T(8,128)(2,1)}, u32[]{:S(2)}, u32[]{:S(2)}) collective-permute-start(bf16[192,3840]{1,0:T(8,128)(2,1)S(1)} %copy-done.13), channel_id=1, source_target_pairs={{0,4},{2,6},{4,0},{6,2},{8,12},{10,14},{12,8},{14,10},{16,20},{18,... | collective-permute-start | bytes 4423688 | tf_op jit(solution)/shard_map/ppermute | solution.py:73
  494.3 34.0 %collective-permute-start.30 = (bf16[192,3840]{1,0:T(8,128)(2,1)S(1)}, bf16[192,3840]{1,0:T(8,128)(2,1)S(1)}, u32[]{:S(2)}, u32[]{:S(2)}) collective-permute-start(bf16[192,3840]{1,0:T(8,128)(2,1)S(1)} %copy-done.11), channel_id=1, source_target_pairs={{0,2},{2,0},{4,6},{6,4},{8,10},{10,8},{12,14},{14,12},{16,18},{18,... | collective-permute-start | bytes 4423688 | tf_op jit(solution)/shard_map/ppermute | solution.py:73
  525.2 33.1 %collective-permute-start.31 = (bf16[192,3840]{1,0:T(8,128)(2,1)S(1)}, bf16[192,3840]{1,0:T(8,128)(2,1)}, u32[]{:S(2)}, u32[]{:S(2)}) collective-permute-start(bf16[192,3840]{1,0:T(8,128)(2,1)S(1)} %copy-done.11), channel_id=1, source_target_pairs={{0,4},{2,6},{4,0},{6,2},{8,12},{10,14},{12,8},{14,10},{16,20},{18,... | collective-permute-start | bytes 4423688 | tf_op jit(solution)/shard_map/ppermute | solution.py:73
  528.3 34.4 %collective-permute-start.8 = (bf16[192,5376]{1,0:T(8,128)(2,1)S(1)}, bf16[192,5376]{1,0:T(8,128)(2,1)S(1)}, u32[]{:S(2)}, u32[]{:S(2)}) collective-permute-start(bf16[192,5376]{1,0:T(8,128)(2,1)S(1)} %copy-done.9), channel_id=1, source_target_pairs={{0,2},{2,0},{4,6},{6,4},{8,10},{10,8},{12,14},{14,12},{16,18},{18,... | collective-permute-start | bytes 6193160 | tf_op jit(solution)/shard_map/ppermute | solution.py:73
  558.3 8.9 %collective-permute-start.10 = (bf16[192,5376]{1,0:T(8,128)(2,1)}, bf16[192,5376]{1,0:T(8,128)(2,1)S(1)}, u32[]{:S(2)}, u32[]{:S(2)}) collective-permute-start(bf16[192,5376]{1,0:T(8,128)(2,1)} %collective-permute-done.9), channel_id=1, source_target_pairs={{0,2},{2,0},{4,6},{6,4},{8,10},{10,8},{12,14},{14,12},{16,18},{18,... | collective-permute-start | bytes 6193160 | tf_op jit(solution)/shard_map/ppermute | solution.py:73
  559.9 9.3 %copy-start.2 = (bf16[4,192,3840]{2,1,0:T(8,128)(2,1)}, bf16[4,192,3840]{2,1,0:T(8,128)(2,1)S(1)}, u32[]{:S(2)}) copy-start(bf16[4,192,3840]{2,1,0:T(8,128)(2,1)S(1)} %bitcast_dynamic-update-slice_fusion.17) | copy-start | bytes 17694724
  559.9 15.4 %collective-permute-start.14 = (bf16[192,5376]{1,0:T(8,128)(2,1)}, bf16[192,5376]{1,0:T(8,128)(2,1)S(1)}, u32[]{:S(2)}, u32[]{:S(2)}) collective-permute-start(bf16[192,5376]{1,0:T(8,128)(2,1)} %collective-permute-done.13), channel_id=1, source_target_pairs={{0,2},{2,0},{4,6},{6,4},{8,10},{10,8},{12,14},{14,12},{16,18},{18,... | collective-permute-start | bytes 6193160 | tf_op jit(solution)/shard_map/ppermute | solution.py:73
  560.5 10.2 %collective-permute-start.12 = (bf16[192,5376]{1,0:T(8,128)(2,1)S(1)}, bf16[192,5376]{1,0:T(8,128)(2,1)S(1)}, u32[]{:S(2)}, u32[]{:S(2)}) collective-permute-start(bf16[192,5376]{1,0:T(8,128)(2,1)S(1)} %collective-permute-done.11), channel_id=1, source_target_pairs={{0,2},{2,0},{4,6},{6,4},{8,10},{10,8},{12,14},{14,12},{16,18},{18,... | collective-permute-start | bytes 6193160 | tf_op jit(solution)/shard_map/ppermute | solution.py:73
  560.5 17.7 %collective-permute-start.16 = (bf16[192,5376]{1,0:T(8,128)(2,1)S(1)}, bf16[192,5376]{1,0:T(8,128)(2,1)S(1)}, u32[]{:S(2)}, u32[]{:S(2)}) collective-permute-start(bf16[192,5376]{1,0:T(8,128)(2,1)S(1)} %collective-permute-done.15), channel_id=1, source_target_pairs={{0,2},{2,0},{4,6},{6,4},{8,10},{10,8},{12,14},{14,12},{16,18},{18,... | collective-permute-start | bytes 6193160 | tf_op jit(solution)/shard_map/ppermute | solution.py:73
  562.7 170.7 %collective-permute-start.23 = (bf16[192,3840]{1,0:T(8,128)(2,1)}, bf16[192,3840]{1,0:T(8,128)(2,1)}, u32[]{:S(2)}, u32[]{:S(2)}) collective-permute-start(bf16[192,3840]{1,0:T(8,128)(2,1)} %collective-permute-done.22), channel_id=1, source_target_pairs={{0,2},{2,0},{4,6},{6,4},{8,10},{10,8},{12,14},{14,12},{16,18},{18,... | collective-permute-start | bytes 4423688 | tf_op jit(solution)/shard_map/ppermute | solution.py:73
  567.2 145.4 %collective-permute-start.28 = (bf16[192,3840]{1,0:T(8,128)(2,1)}, bf16[192,3840]{1,0:T(8,128)(2,1)}, u32[]{:S(2)}, u32[]{:S(2)}) collective-permute-start(bf16[192,3840]{1,0:T(8,128)(2,1)} %collective-permute-done.27), channel_id=1, source_target_pairs={{0,2},{2,0},{4,6},{6,4},{8,10},{10,8},{12,14},{14,12},{16,18},{18,... | collective-permute-start | bytes 4423688 | tf_op jit(solution)/shard_map/ppermute | solution.py:73
  570.7 150.0 %collective-permute-start.32 = (bf16[192,3840]{1,0:T(8,128)(2,1)}, bf16[192,3840]{1,0:T(8,128)(2,1)}, u32[]{:S(2)}, u32[]{:S(2)}) collective-permute-start(bf16[192,3840]{1,0:T(8,128)(2,1)} %collective-permute-done.31), channel_id=1, source_target_pairs={{0,2},{2,0},{4,6},{6,4},{8,10},{10,8},{12,14},{14,12},{16,18},{18,... | collective-permute-start | bytes 4423688 | tf_op jit(solution)/shard_map/ppermute | solution.py:73
  676.5 8.1 copy-start.15
  676.5 8.1 copy-start.16
  691.8 4.8 copy-start.7
  701.7 11.0 %slice-start.4 = ((s8[5898240]{0:T(1024)(128)(4,1)}), s8[4194304]{0:T(1024)(128)(4,1)S(1)}, s32[]{:S(2)}) async-start(s8[5898240]{0:T(1024)(128)(4,1)} %bitcast.121), calls=%async_computation.4 | async-start | bytes 8388608
  701.7 12.7 %slice-start.6 = ((s8[6291456]{0:T(1024)(128)(4,1)}), s8[4194304]{0:T(1024)(128)(4,1)S(1)}, s32[]{:S(2)}) async-start(s8[6291456]{0:T(1024)(128)(4,1)} %bitcast.133), calls=%async_computation.6 | async-start | bytes 8388608
  702.0 10.7 %slice-start.5 = ((s8[5898240]{0:T(1024)(128)(4,1)}), s8[1703936]{0:T(1024)(128)(4,1)S(1)}, s32[]{:S(2)}) async-start(s8[5898240]{0:T(1024)(128)(4,1)} %bitcast.121), calls=%async_computation.5 | async-start | bytes 3407872
  702.0 12.4 %slice-start.7 = ((s8[6291456]{0:T(1024)(128)(4,1)}), s8[2097152]{0:T(1024)(128)(4,1)S(1)}, s32[]{:S(2)}) async-start(s8[6291456]{0:T(1024)(128)(4,1)} %bitcast.133), calls=%async_computation.7 | async-start | bytes 4194304
  712.7 8.0 slice-start
  714.4 6.3 slice-start.1
  720.7 12.7 %slice-start.2 = ((s8[5898240]{0:T(1024)(128)(4,1)}), s8[4194304]{0:T(1024)(128)(4,1)S(1)}, s32[]{:S(2)}) async-start(s8[5898240]{0:T(1024)(128)(4,1)} %bitcast.118), calls=%async_computation.2 | async-start | bytes 8388608
  720.7 14.3 %slice-start.8 = ((s8[6291456]{0:T(1024)(128)(4,1)}), s8[4194304]{0:T(1024)(128)(4,1)S(1)}, s32[]{:S(2)}) async-start(s8[6291456]{0:T(1024)(128)(4,1)} %bitcast.135), calls=%async_computation.8 | async-start | bytes 8388608
  722.4 11.0 %slice-start.3 = ((s8[5898240]{0:T(1024)(128)(4,1)}), s8[1703936]{0:T(1024)(128)(4,1)S(1)}, s32[]{:S(2)}) async-start(s8[5898240]{0:T(1024)(128)(4,1)} %bitcast.118), calls=%async_computation.3 | async-start | bytes 3407872
  722.4 12.6 %slice-start.9 = ((s8[6291456]{0:T(1024)(128)(4,1)}), s8[2097152]{0:T(1024)(128)(4,1)S(1)}, s32[]{:S(2)}) async-start(s8[6291456]{0:T(1024)(128)(4,1)} %bitcast.135), calls=%async_computation.9 | async-start | bytes 4194304
  731.8 37.3 %collective-permute-start.33 = (bf16[1024,768]{0,1:T(8,128)(2,1)S(1)}, bf16[1024,768]{0,1:T(8,128)(2,1)S(1)}, u32[]{:S(2)}, u32[]{:S(2)}) collective-permute-start(bf16[1024,768]{0,1:T(8,128)(2,1)S(1)} %get-tuple-element.21), channel_id=1, source_target_pairs={{0,1},{1,0},{2,3},{3,2},{4,5},{5,4},{6,7},{7,6},{8,9},{9,8},{10,11... | collective-permute-start | bytes 4718600 | tf_op jit(solution)/shard_map/ppermute | solution.py:73
  741.3 61.1 %collective-permute-start.24 = (bf16[1024,768]{0,1:T(8,128)(2,1)S(1)}, bf16[1024,768]{0,1:T(8,128)(2,1)S(1)}, u32[]{:S(2)}, u32[]{:S(2)}) collective-permute-start(bf16[1024,768]{0,1:T(8,128)(2,1)S(1)} %get-tuple-element.23), channel_id=1, source_target_pairs={{0,1},{1,0},{2,3},{3,2},{4,5},{5,4},{6,7},{7,6},{8,9},{9,8},{10,11... | collective-permute-start | bytes 4718600 | tf_op jit(solution)/shard_map/ppermute | solution.py:73
  771.1 37.5 %collective-permute-start.34 = (bf16[512,768]{0,1:T(8,128)(2,1)}, bf16[512,768]{0,1:T(8,128)(2,1)}, u32[]{:S(2)}, u32[]{:S(2)}) collective-permute-start(bf16[512,768]{0,1:T(8,128)(2,1)} %slice.57), channel_id=1, source_target_pairs={{0,8},{2,10},{4,12},{6,14},{8,0},{10,2},{12,4},{14,6},{16,24},{18,... | collective-permute-start | bytes 2359304 | tf_op jit(solution)/shard_map/ppermute | solution.py:73
  806.0 19.4 %collective-permute-start.35 = (bf16[512,768]{0,1:T(8,128)(2,1)}, bf16[512,768]{0,1:T(8,128)(2,1)}, u32[]{:S(2)}, u32[]{:S(2)}) collective-permute-start(bf16[512,768]{0,1:T(8,128)(2,1)} %slice.56), channel_id=1, source_target_pairs={{0,8},{2,10},{4,12},{6,14},{8,0},{10,2},{12,4},{14,6},{16,24},{18,... | collective-permute-start | bytes 2359304 | tf_op jit(solution)/shard_map/ppermute | solution.py:73
  808.6 18.2 %copy-start.1 = (bf16[512,1536]{0,1:T(8,128)(2,1)S(1)}, bf16[512,1536]{0,1:T(8,128)(2,1)}, u32[]{:S(2)}) copy-start(bf16[512,1536]{0,1:T(8,128)(2,1)} %copy.17) | copy-start | bytes 4718596
  (2 other events, 2.8 us)

commit v2 on v0

v2 whole, which is shorter than its diff:
```python
import jax
import jax.numpy as jnp
from jax import lax
from jax.experimental import pallas as pl
from jax.experimental.pallas import tpu as pltpu
from jax.sharding import PartitionSpec as P

HD = 128
PATCHES = 256


def layer_norm(values, gain):
    mean = jnp.mean(values, axis=-1, keepdims=True)
    centred = values - mean
    variance = jnp.mean(centred * centred, axis=-1, keepdims=True)
    return centred * lax.rsqrt(variance + 1e-06) * gain


def attention(projected, q_gain, k_gain):
    tok_count = projected[0].shape[0]
    heads = q_gain.shape[0]
    images = tok_count // PATCHES
    queries = layer_norm(projected[0].reshape(tok_count, heads, HD), q_gain)
    keys = layer_norm(projected[1].reshape(tok_count, heads, HD), k_gain)
    split = (images, PATCHES, heads, HD)
    queries = queries.astype(jnp.bfloat16).reshape(split)
    keys = keys.astype(jnp.bfloat16).reshape(split)
    values = projected[2].astype(jnp.bfloat16).reshape(split)
    scores = jnp.einsum(
        "iqhd,ikhd->ihqk", queries, keys, preferred_element_type=jnp.float32
    ) * HD ** (-0.5)
    scores = scores - jnp.max(scores, axis=-1, keepdims=True)
    weights = jnp.exp(scores)
    probs = (weights / jnp.sum(weights, axis=-1, keepdims=True)).astype(jnp.bfloat16)
    attended = jnp.einsum("ihqk,ikhd->iqhd", probs, values, preferred_element_type=jnp.float32)
    return attended.astype(jnp.bfloat16).reshape(tok_count, heads * HD)


def gathered(tokens, ln_gain, w_qkv, w_up, q_gain, k_gain, w_proj, w_down):
    rows = tokens.astype(jnp.float32)
    panels = lax.all_gather(tokens, "mp", axis=1, tiled=True)
    normed = layer_norm(panels.astype(jnp.float32), ln_gain).astype(jnp.bfloat16)
    projected = jnp.einsum(
        "td,dca->cta",
        normed,
        lax.all_gather(w_qkv, "fsdp", axis=0, tiled=True),
        preferred_element_type=jnp.float32,
    )
    hidden_pre = jnp.dot(
        normed,
        lax.all_gather(w_up, "fsdp", axis=0, tiled=True),
        preferred_element_type=jnp.float32,
    )
    attended = attention(projected, q_gain, k_gain)
    activated = jax.nn.gelu(hidden_pre, approximate=False).astype(jnp.bfloat16)
    joined = jnp.concatenate([attended, activated], axis=1)
    out_rows = jnp.concatenate([w_proj, w_down], axis=0)
    terms = jnp.dot(
        joined,
        lax.all_gather(out_rows, "fsdp", axis=1, tiled=True),
        preferred_element_type=jnp.float32,
    )
    branches = lax.psum_scatter(
        terms.astype(jnp.bfloat16), "mp", scatter_dimension=1, tiled=True
    ).astype(jnp.float32)
    return (rows + branches).astype(jnp.bfloat16)


def flip(z, k):
    if k == 1:
        return z + 1 - 2 * lax.rem(z, 2)
    if k == 2:
        return z + 2 - 4 * lax.div(z, 2)
    return 3 - z if k == 3 else z


def fused_kernel(
    tokens_ref, gain_ref, qgain_ref, kgain_ref, qkv_ref, up_ref, out_ref,
    terms_ref, all_qkv, all_up, all_out,
    panels, normed, projected, joined, in_tile, out_tile,
    send_sem, recv_sem, local_sem, tile_sem,
):
    me, side = lax.axis_index("fsdp"), lax.axis_index("mp")
    z, y, c = lax.div(me, 4), lax.rem(lax.div(me, 2), 2), lax.rem(me, 2)
    half = lax.rem(z, 2)
    rows = tokens_ref.shape[0]
    depth = up_ref.shape[0]
    heads = qgain_ref.shape[0] // 2
    head_cols = heads * HD
    hidden = up_ref.shape[1] // 2
    tall = 2 * rows
    width = in_tile.shape[2]

    def device(z, y, c):
        return (z * 4 + y * 2 + c, side)

    def remote(index, src, dst, target):
        return pltpu.make_async_remote_copy(
            src_ref=src,
            dst_ref=dst,
            send_sem=send_sem.at[index],
            recv_sem=recv_sem.at[index],
            device_id=target,
            device_id_type=pl.DeviceIdType.MESH,
        )

    def slot(ref, z, y, c):
        return ref.at[pl.ds(pl.multiple_of((z * 4 + y * 2 + c) * depth, depth), depth)]

    partners = [device(flip(z, k), y, c) for k in (1, 2, 3)]
    partners += [device(z, 1 - y, c), device(z, y, 1 - c), (me, 1 - side)]
    barrier = pltpu.get_barrier_semaphore()
    for partner in partners:
        pl.semaphore_signal(
            barrier, inc=1, device_id=partner, device_id_type=pl.DeviceIdType.MESH
        )
    pl.semaphore_wait(barrier, len(partners))

    wholes = (all_qkv, all_up, all_out)

    def part(t, which):
        if t == 1:
            return up_ref.at[:, pl.ds(pl.multiple_of(which * hidden, 128), hidden)]
        return (qkv_ref, None, out_ref)[t].at[which]

    copies = {}
    for t in range(3):
        base = 15 * t
        mine = slot(wholes[t], z, y, c)
        for k in range(4):
            if k:
                copies["z", t, k] = remote(
                    base + k - 1, part(t, 1 - half if k % 2 else half), mine, device(flip(z, k), y, c)
                )
            here = slot(wholes[t], flip(z, k), y, c)
            source = part(t, half) if k == 0 else here
            copies["y", t, k] = remote(base + 3 + k, source, here, device(z, 1 - y, c))
            copies["c", t, k, 0] = remote(base + 7 + k, source, here, device(z, y, 1 - c))
            across = slot(wholes[t], flip(z, k), 1 - y, c)
            copies["c", t, k, 1] = remote(base + 11 + k, across, across, device(z, y, 1 - c))
    near, far = pl.ds(0, rows), pl.ds(rows, rows)
    copies["tz"] = remote(45, tokens_ref, panels.at[side, far], device(flip(z, 1), y, c))
    copies["tx", 0] = remote(46, tokens_ref, panels.at[side, near], (me, 1 - side))
    copies["tx", 1] = remote(47, panels.at[side, far], panels.at[side, far], (me, 1 - side))

    def start(*keys):
        for key in keys:
            copies[key].start()

    def arrived(*keys):
        for key in keys:
            copies[key].wait_recv()

    def forward_z(t, k):
        arrived(("z", t, k))
        start(("y", t, k), ("c", t, k, 0))

    def forward_y(t, k):
        arrived(("y", t, k))
        start(("c", t, k, 1))

    def landed(t, k):
        arrived(("c", t, k, 0), ("c", t, k, 1))

    def stream(first, count, tiles, source, body):
        def fetch(step):
            which = lax.rem(step, 2)
            return pltpu.make_async_copy(source(step), tiles.at[which], tile_sem.at[which])

        fetch(first).start()

        def step(i, _):
            @pl.when(i + 1 < first + count)
            def _():
                fetch(i + 1).start()

            fetch(i).wait()
            body(i, tiles[lax.rem(i, 2)])
            return 0

        lax.fori_loop(first, first + count, step, 0)

    def by_rows(run, size):
        def step(i, _):
            run(pl.ds(pl.multiple_of(i * size, size), size))
            return 0

        lax.fori_loop(0, tall // size, step, 0)

    def columns(step):
        return pl.ds(pl.multiple_of(step * width, width), width)

    def project(first, count):
        def body(step, tile):
            def run(at):
                projected[at, columns(step)] = jnp.dot(
                    normed[at, :], tile, preferred_element_type=jnp.float32
                )

            by_rows(run, 512)

        stream(first, count, in_tile, lambda i: all_qkv.at[:, columns(i)], body)

    def expand(first, count):
        def body(step, tile):
            def run(at):
                pre = jnp.dot(normed[at, :], tile, preferred_element_type=jnp.float32)
                active = 0.5 * pre * (1.0 + lax.erf(pre * 0.5**0.5))
                into = pl.ds(pl.multiple_of(head_cols + step * width, width), width)
                joined[at, into] = active.astype(jnp.bfloat16)

            by_rows(run, 512)

        stream(first, count, in_tile, lambda i: all_up.at[:, columns(i)], body)

    def reduce(k):
        tile_rows = out_tile.shape[1]

        def source(i):
            begin = flip(z, k) * (4 * depth) + i * tile_rows
            return all_out.at[pl.ds(pl.multiple_of(begin, tile_rows), tile_rows)]

        def body(step, tile):
            into = pl.ds(pl.multiple_of(step * tile_rows, tile_rows), tile_rows)

            def run(at):
                terms_ref[k, at, into] = lax.dot_general(
                    joined[at, :], tile, (((1,), (1,)), ((), ())),
                    preferred_element_type=jnp.float32,
                ).astype(jnp.bfloat16)

            by_rows(run, 512)

        stream(0, 4 * depth // tile_rows, out_tile, source, body)

    def attend(first, count):
        def step(i, _):
            image, head = lax.div(i, heads), lax.rem(i, heads)
            at = pl.ds(pl.multiple_of(image * PATCHES, PATCHES), PATCHES)

            def pick(group):
                begin = pl.multiple_of(group * head_cols + head * HD, HD)
                return projected[at, pl.ds(begin, HD)]

            one = pl.ds(half * heads + head, 1)
            queries = layer_norm(pick(0), qgain_ref[one, :]).astype(jnp.bfloat16)
            keys = layer_norm(pick(1), kgain_ref[one, :]).astype(jnp.bfloat16)
            values = pick(2).astype(jnp.bfloat16)
            scores = lax.dot_general(
                queries, keys, (((1,), (1,)), ((), ())), preferred_element_type=jnp.float32
            ) * HD ** (-0.5)
            weights = jnp.exp(scores - jnp.max(scores, axis=-1, keepdims=True))
            probs = weights / jnp.sum(weights, axis=-1, keepdims=True)
            mixed = jnp.dot(
                probs.astype(jnp.bfloat16), values, preferred_element_type=jnp.float32
            )
            joined[at, pl.ds(pl.multiple_of(head * HD, HD), HD)] = mixed.astype(jnp.bfloat16)
            return 0

        lax.fori_loop(first, first + count, step, 0)

    def normalise():
        def run(at):
            left = panels[0, at, :].astype(jnp.float32)
            right = panels[1, at, :].astype(jnp.float32)
            total = jnp.sum(left, axis=-1, keepdims=True) + jnp.sum(right, axis=-1, keepdims=True)
            cols = panels.shape[2]
            mean = total / (2 * cols)
            left, right = left - mean, right - mean
            square = jnp.sum(left * left, axis=-1, keepdims=True)
            square = square + jnp.sum(right * right, axis=-1, keepdims=True)
            scale = lax.rsqrt(square / (2 * cols) + 1e-06)
            normed[at, :cols] = (left * scale * gain_ref[:, :cols]).astype(jnp.bfloat16)
            normed[at, cols:] = (right * scale * gain_ref[:, cols:]).astype(jnp.bfloat16)

        by_rows(run, 64)

    locals_ = [
        pltpu.make_async_copy(part(t, half), slot(wholes[t], z, y, c), local_sem.at[t])
        for t in range(3)
    ]
    locals_.append(
        pltpu.make_async_copy(tokens_ref, panels.at[side, near], local_sem.at[3])
    )

    qkv_steps, up_steps = 3 * head_cols // width, hidden // width
    tiles_of_heads = heads * (tall // PATCHES)

    start("tz", ("tx", 0), ("z", 0, 1), ("z", 0, 2), ("z", 0, 3))
    start(("y", 0, 0), ("c", 0, 0, 0), ("y", 1, 0), ("y", 2, 0), ("c", 1, 0, 0), ("c", 2, 0, 0))
    for copy in locals_:
        copy.start()
    arrived("tz")
    start(("tx", 1))
    forward_y(0, 0)
    for k in (1, 2, 3):
        forward_z(0, k)
    start(("z", 1, 1), ("z", 1, 2))
    for copy in locals_:
        copy.wait()
    arrived(("tx", 0), ("tx", 1))
    normalise()
    forward_y(1, 0)
    forward_y(2, 0)
    for k in (1, 2):
        forward_z(1, k)
    start(("z", 1, 3), ("z", 2, 1))
    for k in (1, 2, 3):
        forward_y(0, k)
    for k in range(4):
        landed(0, k)
    project(0, qkv_steps)
    attend(0, tiles_of_heads // 2)
    forward_z(1, 3)
    start(("z", 2, 2))
    forward_z(2, 1)
    forward_y(1, 1)
    forward_y(1, 2)
    attend(tiles_of_heads // 2, tiles_of_heads - tiles_of_heads // 2)
    forward_y(1, 3)
    for k in range(4):
        landed(1, k)
    expand(0, up_steps // 2)
    forward_z(2, 2)
    start(("z", 2, 3))
    forward_y(2, 1)
    expand(up_steps // 2, up_steps - up_steps // 2)
    for k in (0, 1):
        landed(2, k)
        reduce(k)
    forward_y(2, 2)
    landed(2, 2)
    reduce(2)
    forward_z(2, 3)
    forward_y(2, 3)
    landed(2, 3)
    reduce(3)
    for copy in copies.values():
        copy.wait_send()


def fused(tokens, ln_gain, w_qkv, w_up, q_gain, k_gain, w_proj, w_down):
    side = lax.axis_index("mp")
    me = lax.axis_index("fsdp")
    z = me // 4
    half = z % 2
    rows, cols = tokens.shape
    depth = w_up.shape[0]
    heads = q_gain.shape[0] // 2
    head_cols, hidden = heads * HD, w_up.shape[1] // 2
    tall, whole, joint = 2 * rows, 16 * depth, head_cols + hidden
    qkv = w_qkv.reshape(depth, 3, 2, head_cols).transpose(2, 0, 1, 3)
    qkv = qkv.reshape(2, depth, 3 * head_cols)
    outs = jnp.concatenate(
        [w_proj.reshape(2, head_cols, depth), w_down.reshape(2, hidden, depth)], axis=1
    ).transpose(0, 2, 1)
    bf16, f32 = jnp.bfloat16, jnp.float32
    anywhere, vmem = pl.BlockSpec(memory_space=pl.ANY), pl.BlockSpec(memory_space=pltpu.VMEM)
    terms = pl.pallas_call(
        fused_kernel,
        out_shape=[
            jax.ShapeDtypeStruct((4, tall, 4 * depth), bf16),
            jax.ShapeDtypeStruct((whole, 3 * head_cols), bf16),
            jax.ShapeDtypeStruct((whole, hidden), bf16),
            jax.ShapeDtypeStruct((whole, joint), bf16),
        ],
        in_specs=[anywhere, vmem, vmem, vmem, anywhere, anywhere, anywhere],
        out_specs=[vmem, anywhere, anywhere, anywhere],
        scratch_shapes=[
            pltpu.VMEM((2, tall, cols), bf16),
            pltpu.VMEM((tall, 2 * cols), bf16),
            pltpu.VMEM((tall, 3 * head_cols), f32),
            pltpu.VMEM((tall, joint), bf16),
            pltpu.VMEM((2, whole, 256), bf16),
            pltpu.VMEM((2, 256, joint), bf16),
            pltpu.SemaphoreType.DMA((48,)),
            pltpu.SemaphoreType.DMA((48,)),
            pltpu.SemaphoreType.DMA((4,)),
            pltpu.SemaphoreType.DMA((2,)),
        ],
        compiler_params=pltpu.CompilerParams(
            collective_id=0, has_side_effects=True, vmem_limit_bytes=58 * 2**20
        ),
    )(tokens, ln_gain[None], q_gain, k_gain, qkv, w_up, outs)[0]

    def swap(value, mask, axis="fsdp"):
        count = 16 if axis == "fsdp" else 2
        return lax.ppermute(value, axis, [(i, i ^ mask) for i in range(count)])

    keep_low = z // 2 == side
    own, far = [], []
    for stage in range(2):
        low, high = terms[stage], terms[stage + 2]
        keep = jnp.where(keep_low, low, high)
        got = swap(jnp.where(keep_low, high, low), 1, "mp")
        total = keep.astype(f32) + got.astype(f32)
        own.append(total[:rows])
        far.append(swap(total[rows:].astype(bf16), 4))
    done = [own[s] + far[1 - s].astype(f32) for s in range(2)]
    branches = jnp.where(
        half == 0, jnp.concatenate(done, axis=1), jnp.concatenate(done[::-1], axis=1)
    )
    return (tokens.astype(f32) + branches).astype(bf16)


def solution(mesh):
    n, sides = mesh.shape["fsdp"], mesh.shape["mp"]
    return jax.shard_map(
        fused if (n, sides) == (16, 2) else gathered,
        mesh=mesh,
        in_specs=(
            P("fsdp", "mp"),
            P(),
            P("fsdp", None, "mp"),
            P("fsdp", "mp"),
            P("mp", None),
            P("mp", None),
            P("mp", "fsdp"),
            P("mp", "fsdp"),
        ),
        out_specs=P("fsdp", "mp"),
        check_vma=False,
    )
```

time: 710 us -> 511 us (0.72)
  waiting for transfers between devices: 538 us -> 98.9 us
  Pallas kernels: 0 us -> 361 us
  matrix products: 106 us -> 0 us
  starting transfers between devices: 0.16 us -> 22.8 us
  other arithmetic: 25.2 us -> 10.8 us
  between operations: 13.3 us -> 0.09 us
  local copies, waits for them, and re-layouts: 26.9 us -> 16.4 us
    all_gather x4 -> x0, waiting for transfers between devices: 493 us -> none  [the longest x1 182 us: local(): lax.all_gather(out_rows, 'fsdp', axis=1, tiled=True)]
    pallas_call x0 -> x1, Pallas kernels: none -> 361 us  [fused(): pl.pallas_call(fused_kernel, out_shape=[jax.ShapeDtypeStruct((4, tall, 4...]
    dot_general x5 -> x0, matrix products: 106 us -> none  [the longest x1 51.8 us: local(): jnp.dot(columns, lax.all_gather(w_up, 'fsdp', axis=0, tiled=True), prefer...]
    ppermute x0 -> x4, waiting for transfers between devices: none -> 98.9 us  [swap(): return lax.ppermute(value, axis, [(i, i ^ mask) for i in range(count)])]
    reduce_scatter x1 -> x0, waiting for transfers between devices: 43.5 us -> none  [local(): lax.psum_scatter(terms.astype(jnp.bfloat16), 'mp', scatter_dimension=1, t...]
    ppermute x0 -> x4, starting transfers between devices: none -> 22.8 us  [swap(): return lax.ppermute(value, axis, [(i, i ^ mask) for i in range(count)])]
    reshape x1 -> x5, local copies, waits for them, and re-layouts: 4.6 us -> 14.3 us  [the longest x2 7.81 us: fused(): qkv = w_qkv.reshape(depth, 3, 2, head_cols).transpose(2, 0, 1, 3)]
    convert_element_type x2 -> x1, other arithmetic: 10.6 us -> 1.67 us  [fused(): return (tokens.astype(f32) + branches).astype(bf16)]
  transfers between devices with their start and end apart: 5 -> 4, of which waited for: 5 -> 4; matrix products, arithmetic and copies ran while one was open for 17% -> 1% of each run, Pallas kernels for 0% -> 0%
where the time goes in v2:
time: 511 us; the launch traced here: 510 us
  Pallas kernels  361 us (71%)
  waiting for transfers between devices  98.9 us (19%)
  starting transfers between devices  22.8 us (4%)
  local copies, waits for them, and re-layouts  16.4 us (3%)
  other arithmetic  10.8 us (2%)
    pallas_call x1, Pallas kernels, fused(): pl.pallas_call(fused_kernel, out_shape=[jax.ShapeDtypeStruct((4, tall, 4...  361 us
    ppermute x4, waiting for transfers between devices, swap(): return lax.ppermute(value, axis, [(i, i ^ mask) for i in range(count)])  98.9 us
    ppermute x4, starting transfers between devices, swap(): return lax.ppermute(value, axis, [(i, i ^ mask) for i in range(count)])  22.8 us
  transfers between devices with their start and end apart: 4, of which 4 were waited for; matrix products, arithmetic and copies ran while one was open for 1% of the time, Pallas kernels for 0%

profile of v2, /device:TPU:0, one launch (start us, length us, event | category | flops | bytes accessed | tf_op | source)
XLA Modules:
  0.0 510.1 jit_solution(16203286298652271301)
XLA Ops:
  0.0 1.1 copy.20
  1.1 4.8 reshape.24
  5.9 3.0 copy.19
  8.9 3.6 reshape.25.qkv_ref
  12.5 1.8 copy.18
  14.3 1.8 maximum_bitcast_fusion.out_ref
  16.1 361.2 %shard_map.82 = (bf16[4,1024,768]{2,1,0:T(8,128)(2,1)}, bf16[3072,2304]{1,0:T(8,128)(2,1)}, bf16[3072,3072]{1,0:T(8,128)(2,1)}, bf16[3072,3840]{1,0:T(8,128)(2,1)}) custom-call(bf16[512,1536]{1,0:T(8,128)(2,1)} %tokens_ref.1, f32[1,3072]{1,0:T(1,128)} %bitcast.31, f32[12,128]{1,0:T(8,128)} %qgain_ref.1, f32[12,128]{1,0:T(8,128)} %kgain_ref.1, ...), custom_call_target="tpu_custom_call" | custom-call | tf_op jit(solution)/shard_map/pallas_call | solution.py:359
  377.3 0.0 copy-start
  377.3 3.3 select_bitcast_fusion.1
  380.6 1.6 collective-permute-start
  382.2 0.5 collective-permute-start.1
  382.7 35.3 %collective-permute-done = bf16[1024,768]{1,0:T(8,128)(2,1)S(1)} collective-permute-done((bf16[1024,768]{1,0:T(8,128)(2,1)S(1)}, bf16[1024,768]{1,0:T(8,128)(2,1)S(1)}, u32[]{:S(2)}, u32[]{:S(2)}) %collective-permute-start) | collective-permute-done | bytes 1572896 | tf_op jit(solution)/shard_map/ppermute | solution.py:388
  418.0 31.7 %collective-permute-done.1 = bf16[1024,768]{1,0:T(8,128)(2,1)S(1)} collective-permute-done((bf16[1024,768]{1,0:T(8,128)(2,1)S(1)}, bf16[1024,768]{1,0:T(8,128)(2,1)S(1)}, u32[]{:S(2)}, u32[]{:S(2)}) %collective-permute-start.1) | collective-permute-done | bytes 1572896 | tf_op jit(solution)/shard_map/ppermute | solution.py:388
  449.7 0.0 copy-done
  449.7 1.0 convert_add_fusion.1
  450.8 0.0 copy-start.1
  450.8 1.1 slice.51
  451.9 20.0 %collective-permute-start.2 = (bf16[512,768]{1,0:T(8,128)(2,1)}, bf16[512,768]{1,0:T(8,128)(2,1)}, u32[]{:S(2)}, u32[]{:S(2)}) collective-permute-start(bf16[512,768]{1,0:T(8,128)(2,1)} %slice.51), channel_id=1, source_target_pairs={{0,8},{2,10},{4,12},{6,14},{8,0},{10,2},{12,4},{14,6},{16,24},{18,... | collective-permute-start | bytes 2359304 | tf_op jit(solution)/shard_map/ppermute | solution.py:388
  471.8 0.0 copy-done.1
  471.8 1.0 slice.50
  472.8 0.8 collective-permute-start.3
  473.5 17.0 %collective-permute-done.2 = bf16[512,768]{1,0:T(8,128)(2,1)} collective-permute-done((bf16[512,768]{1,0:T(8,128)(2,1)}, bf16[512,768]{1,0:T(8,128)(2,1)}, u32[]{:S(2)}, u32[]{:S(2)}) %collective-permute-start.2) | collective-permute-done | bytes 786464 | tf_op jit(solution)/shard_map/ppermute | solution.py:388
  490.5 1.8 slice_add_fusion.1
  492.3 0.0 copy-start.2
  492.3 14.8 %collective-permute-done.3 = bf16[512,768]{1,0:T(8,128)(2,1)} collective-permute-done((bf16[512,768]{1,0:T(8,128)(2,1)}, bf16[512,768]{1,0:T(8,128)(2,1)}, u32[]{:S(2)}, u32[]{:S(2)}) %collective-permute-start.3) | collective-permute-done | bytes 786464 | tf_op jit(solution)/shard_map/ppermute | solution.py:388
  507.1 1.3 slice_add_fusion
  508.4 0.0 copy-done.2
  508.4 1.7 fusion.1
Async XLA Ops:
  377.3 72.4 %copy-start = (bf16[4,1024,768]{2,1,0:T(8,128)(2,1)S(1)}, bf16[4,1024,768]{2,1,0:T(8,128)(2,1)}, u32[]{:S(2)}) copy-start(bf16[4,1024,768]{2,1,0:T(8,128)(2,1)} %get-tuple-element.6) | copy-start | bytes 18874372
  380.6 37.4 %collective-permute-start = (bf16[1024,768]{1,0:T(8,128)(2,1)S(1)}, bf16[1024,768]{1,0:T(8,128)(2,1)S(1)}, u32[]{:S(2)}, u32[]{:S(2)}) collective-permute-start(bf16[1024,768]{1,0:T(8,128)(2,1)S(1)} %get-tuple-element.9), channel_id=1, source_target_pairs={{0,1},{1,0},{2,3},{3,2},{4,5},{5,4},{6,7},{7,6},{8,9},{9,8},{10,11... | collective-permute-start | bytes 4718600 | tf_op jit(solution)/shard_map/ppermute | solution.py:388
  382.2 67.5 %collective-permute-start.1 = (bf16[1024,768]{1,0:T(8,128)(2,1)S(1)}, bf16[1024,768]{1,0:T(8,128)(2,1)S(1)}, u32[]{:S(2)}, u32[]{:S(2)}) collective-permute-start(bf16[1024,768]{1,0:T(8,128)(2,1)S(1)} %get-tuple-element.10), channel_id=1, source_target_pairs={{0,1},{1,0},{2,3},{3,2},{4,5},{5,4},{6,7},{7,6},{8,9},{9,8},{10,11... | collective-permute-start | bytes 4718600 | tf_op jit(solution)/shard_map/ppermute | solution.py:388
  450.8 21.1 %copy-start.1 = (f32[1024,768]{1,0:T(8,128)}, f32[1024,768]{1,0:T(8,128)S(1)}, u32[]{:S(2)}) copy-start(f32[1024,768]{1,0:T(8,128)S(1)} %get-tuple-element.7) | copy-start | bytes 9437188
  451.9 38.7 %collective-permute-start.2 = (bf16[512,768]{1,0:T(8,128)(2,1)}, bf16[512,768]{1,0:T(8,128)(2,1)}, u32[]{:S(2)}, u32[]{:S(2)}) collective-permute-start(bf16[512,768]{1,0:T(8,128)(2,1)} %slice.51), channel_id=1, source_target_pairs={{0,8},{2,10},{4,12},{6,14},{8,0},{10,2},{12,4},{14,6},{16,24},{18,... | collective-permute-start | bytes 2359304 | tf_op jit(solution)/shard_map/ppermute | solution.py:388
  472.8 34.4 %collective-permute-start.3 = (bf16[512,768]{1,0:T(8,128)(2,1)}, bf16[512,768]{1,0:T(8,128)(2,1)}, u32[]{:S(2)}, u32[]{:S(2)}) collective-permute-start(bf16[512,768]{1,0:T(8,128)(2,1)} %slice.50), channel_id=1, source_target_pairs={{0,8},{2,10},{4,12},{6,14},{8,0},{10,2},{12,4},{14,6},{16,24},{18,... | collective-permute-start | bytes 2359304 | tf_op jit(solution)/shard_map/ppermute | solution.py:388
  492.3 16.1 %copy-start.2 = (bf16[512,1536]{1,0:T(8,128)(2,1)S(1)}, bf16[512,1536]{1,0:T(8,128)(2,1)}, u32[]{:S(2)}) copy-start(bf16[512,1536]{1,0:T(8,128)(2,1)} %tokens_ref.1) | copy-start | bytes 4718596

commit v3 on v2

--- a/solution.py
+++ b/solution.py
@@ -7,6 +7,8 @@
 
 HD = 128
 PATCHES = 256
+LAST_PIECES = 3
+SEMAPHORES = 80
 
 
 def layer_norm(values, gain):
@@ -75,9 +77,9 @@
 
 
 def fused_kernel(
-    tokens_ref, gain_ref, qgain_ref, kgain_ref, qkv_ref, up_ref, out_ref,
-    terms_ref, all_qkv, all_up, all_out,
-    panels, normed, projected, joined, in_tile, out_tile,
+    tokens_ref, gain_ref, qgain_ref, kgain_ref, q_ref, k_ref, v_ref, up_ref, outs_ref,
+    block_ref, all_qkv, all_up, all_out,
+    panels, normed, projected, joined, in_tile, out_tile, terms_ref, crossed, passed, summed,
     send_sem, recv_sem, local_sem, tile_sem,
 ):
     me, side = lax.axis_index("fsdp"), lax.axis_index("mp")
@@ -104,9 +106,12 @@
             device_id_type=pl.DeviceIdType.MESH,
         )
 
-    def slot(ref, z, y, c):
-        return ref.at[pl.ds(pl.multiple_of((z * 4 + y * 2 + c) * depth, depth), depth)]
-
+    def slot(t, z, y, c, piece=0, pieces=1):
+        size = depth // pieces
+        begin = (z * 4 + y * 2 + c) * depth + piece * size
+        return wholes[t].at[pl.ds(pl.multiple_of(begin, size), size)]
+
+    wholes = (all_qkv, all_up, all_out)
     partners = [device(flip(z, k), y, c) for k in (1, 2, 3)]
     partners += [device(z, 1 - y, c), device(z, y, 1 - c), (me, 1 - side)]
     barrier = pltpu.get_barrier_semaphore()
@@ -116,32 +121,54 @@
         )
     pl.semaphore_wait(barrier, len(partners))
 
-    wholes = (all_qkv, all_up, all_out)
-
-    def part(t, which):
+    def pieces_of(t, k):
+        return LAST_PIECES if (t, k) == (2, 3) else 1
+
+    def part(t, which, piece=0, pieces=1):
         if t == 1:
             return up_ref.at[:, pl.ds(pl.multiple_of(which * hidden, 128), hidden)]
-        return (qkv_ref, None, out_ref)[t].at[which]
+        size = depth // pieces
+        return outs_ref.at[which, pl.ds(piece * size, size)]
+
+    def thirds(which, into):
+        cols = pl.ds(pl.multiple_of(which * head_cols, 128), head_cols)
+        for g, ref in enumerate((q_ref, k_ref, v_ref)):
+            yield g, ref.at[:, cols], into.at[:, pl.ds(g * head_cols, head_cols)]
 
     copies = {}
+
+    def add(key, src, dst, target):
+        copies[key] = remote(len(copies), src, dst, target)
+
     for t in range(3):
-        base = 15 * t
-        mine = slot(wholes[t], z, y, c)
         for k in range(4):
-            if k:
-                copies["z", t, k] = remote(
-                    base + k - 1, part(t, 1 - half if k % 2 else half), mine, device(flip(z, k), y, c)
-                )
-            here = slot(wholes[t], flip(z, k), y, c)
-            source = part(t, half) if k == 0 else here
-            copies["y", t, k] = remote(base + 3 + k, source, here, device(z, 1 - y, c))
-            copies["c", t, k, 0] = remote(base + 7 + k, source, here, device(z, y, 1 - c))
-            across = slot(wholes[t], flip(z, k), 1 - y, c)
-            copies["c", t, k, 1] = remote(base + 11 + k, across, across, device(z, y, 1 - c))
+            target = device(flip(z, k), y, c)
+            which = 1 - half if k % 2 else half
+            count = pieces_of(t, k)
+            if k and t == 0:
+                for g, src, dst in thirds(which, slot(0, z, y, c)):
+                    add(("z", t, k, g), src, dst, target)
+            for p in range(count):
+                if k and t:
+                    add(("z", t, k, p), part(t, which, p, count), slot(t, z, y, c, p, count), target)
+                here = slot(t, flip(z, k), y, c, p, count)
+                source = part(t, half) if k == 0 and t else here
+                add(("y", t, k, p), source, here, device(z, 1 - y, c))
+                add(("c", t, k, p, 0), source, here, device(z, y, 1 - c))
+                across = slot(t, flip(z, k), 1 - y, c, p, count)
+                add(("c", t, k, p, 1), across, across, device(z, y, 1 - c))
     near, far = pl.ds(0, rows), pl.ds(rows, rows)
-    copies["tz"] = remote(45, tokens_ref, panels.at[side, far], device(flip(z, 1), y, c))
-    copies["tx", 0] = remote(46, tokens_ref, panels.at[side, near], (me, 1 - side))
-    copies["tx", 1] = remote(47, panels.at[side, far], panels.at[side, far], (me, 1 - side))
+    beside, below = (me, 1 - side), device(flip(z, 1), y, c)
+    add("tz", tokens_ref, panels.at[side, far], below)
+    add(("tx", 0), tokens_ref, panels.at[side, near], beside)
+    add(("tx", 1), panels.at[side, far], panels.at[side, far], beside)
+    high = lax.div(z, 2)
+    keep_low = 1 - high - side + 2 * high * side
+    for s in range(2):
+        for r, at in ((0, near), (1, far)):
+            add(("ox", s, r), terms_ref.at[s + 2 * keep_low, at], crossed.at[s, at], beside)
+        add(("oz", s), summed.at[s], passed.at[s], below)
+    assert len(copies) <= SEMAPHORES
 
     def start(*keys):
         for key in keys:
@@ -151,16 +178,20 @@
         for key in keys:
             copies[key].wait_recv()
 
-    def forward_z(t, k):
-        arrived(("z", t, k))
-        start(("y", t, k), ("c", t, k, 0))
-
-    def forward_y(t, k):
-        arrived(("y", t, k))
-        start(("c", t, k, 1))
+    def start_z(t, k):
+        start(*[key for key in copies if key[:3] == ("z", t, k)])
+
+    def forward_z(t, k, p=0):
+        arrived(*[("z", t, k, g) for g in range(3)] if t == 0 else [("z", t, k, p)])
+        start(("y", t, k, p), ("c", t, k, p, 0))
+
+    def forward_y(t, k, p=0):
+        arrived(("y", t, k, p))
+        start(("c", t, k, p, 1))
 
     def landed(t, k):
-        arrived(("c", t, k, 0), ("c", t, k, 1))
+        for p in range(pieces_of(t, k)):
+            arrived(("c", t, k, p, 0), ("c", t, k, p, 1))
 
     def stream(first, count, tiles, source, body):
         def fetch(step):
@@ -213,7 +244,7 @@
 
         stream(first, count, in_tile, lambda i: all_up.at[:, columns(i)], body)
 
-    def reduce(k):
+    def reduce(k, halves=(0, 1)):
         tile_rows = out_tile.shape[1]
 
         def source(i):
@@ -222,16 +253,44 @@
 
         def body(step, tile):
             into = pl.ds(pl.multiple_of(step * tile_rows, tile_rows), tile_rows)
-
-            def run(at):
+            for r in halves:
+                at = (near, far)[r]
                 terms_ref[k, at, into] = lax.dot_general(
                     joined[at, :], tile, (((1,), (1,)), ((), ())),
                     preferred_element_type=jnp.float32,
                 ).astype(jnp.bfloat16)
 
-            by_rows(run, 512)
-
         stream(0, 4 * depth // tile_rows, out_tile, source, body)
+
+    def own_sum(s, at):
+        kept = terms_ref[s + 2 * (1 - keep_low), at, :].astype(jnp.float32)
+        return kept + crossed[s, at, :].astype(jnp.float32)
+
+    def pass_on(s):
+        arrived(("ox", s, 1))
+
+        def step(i, _):
+            begin = pl.multiple_of(i * 128, 128)
+            total = own_sum(s, pl.ds(rows + begin, 128))
+            summed[s, pl.ds(begin, 128), :] = total.astype(jnp.bfloat16)
+            return 0
+
+        lax.fori_loop(0, rows // 128, step, 0)
+        start(("oz", s))
+
+    def finish(s):
+        size = 4 * depth
+        place = half + s - 2 * half * s
+
+        def step(i, _):
+            at = pl.ds(pl.multiple_of(i * 128, 128), 128)
+            cols = pl.ds(pl.multiple_of(place * size, 128), size)
+            total = own_sum(s, at) + passed[1 - s, at, :].astype(jnp.float32)
+            total = panels[side, at, cols].astype(jnp.float32) + total
+            block_ref[at, cols] = total.astype(jnp.bfloat16)
+            return 0
+
+        lax.fori_loop(0, rows // 128, step, 0)
 
     def attend(first, count):
         def step(i, _):
@@ -275,96 +334,115 @@
 
         by_rows(run, 64)
 
-    locals_ = [
-        pltpu.make_async_copy(part(t, half), slot(wholes[t], z, y, c), local_sem.at[t])
-        for t in range(3)
+    own = [pltpu.make_async_copy(tokens_ref, panels.at[side, near], local_sem.at[0])]
+    for t in (1, 2):
+        own.append(pltpu.make_async_copy(part(t, half), slot(t, z, y, c), local_sem.at[t]))
+    first = [
+        pltpu.make_async_copy(src, dst, local_sem.at[3 + g])
+        for g, src, dst in thirds(half, slot(0, z, y, c))
     ]
-    locals_.append(
-        pltpu.make_async_copy(tokens_ref, panels.at[side, near], local_sem.at[3])
-    )
 
     qkv_steps, up_steps = 3 * head_cols // width, hidden // width
-    tiles_of_heads = heads * (tall // PATCHES)
-
-    start("tz", ("tx", 0), ("z", 0, 1), ("z", 0, 2), ("z", 0, 3))
-    start(("y", 0, 0), ("c", 0, 0, 0), ("y", 1, 0), ("y", 2, 0), ("c", 1, 0, 0), ("c", 2, 0, 0))
-    for copy in locals_:
+    quarter = heads * (tall // PATCHES) // 4
+
+    for k in (1, 2, 3):
+        start_z(0, k)
+    start("tz", ("tx", 0))
+    for copy in first + own:
         copy.start()
+    for copy in first:
+        copy.wait()
+    for t in range(3):
+        start(("y", t, 0, 0), ("c", t, 0, 0, 0))
     arrived("tz")
     start(("tx", 1))
     forward_y(0, 0)
-    for k in (1, 2, 3):
-        forward_z(0, k)
-    start(("z", 1, 1), ("z", 1, 2))
-    for copy in locals_:
+    forward_z(0, 1)
+    forward_z(0, 2)
+    start_z(1, 1)
+    start_z(1, 2)
+    forward_z(0, 3)
+    for copy in own:
         copy.wait()
     arrived(("tx", 0), ("tx", 1))
     normalise()
     forward_y(1, 0)
     forward_y(2, 0)
-    for k in (1, 2):
-        forward_z(1, k)
-    start(("z", 1, 3), ("z", 2, 1))
+    forward_z(1, 1)
+    forward_z(1, 2)
+    start_z(1, 3)
+    start_z(2, 1)
     for k in (1, 2, 3):
         forward_y(0, k)
     for k in range(4):
         landed(0, k)
     project(0, qkv_steps)
-    attend(0, tiles_of_heads // 2)
+    attend(0, quarter)
     forward_z(1, 3)
-    start(("z", 2, 2))
+    start_z(2, 2)
     forward_z(2, 1)
     forward_y(1, 1)
     forward_y(1, 2)
-    attend(tiles_of_heads // 2, tiles_of_heads - tiles_of_heads // 2)
+    attend(quarter, 3 * quarter)
     forward_y(1, 3)
     for k in range(4):
         landed(1, k)
     expand(0, up_steps // 2)
     forward_z(2, 2)
-    start(("z", 2, 3))
+    start(("z", 2, 3, 0), ("z", 2, 3, 1))
     forward_y(2, 1)
     expand(up_steps // 2, up_steps - up_steps // 2)
-    for k in (0, 1):
-        landed(2, k)
-        reduce(k)
+    landed(2, 0)
+    reduce(0)
     forward_y(2, 2)
     landed(2, 2)
     reduce(2)
-    forward_z(2, 3)
-    forward_y(2, 3)
+    start(("ox", 0, 1), ("ox", 0, 0))
+    forward_z(2, 3, 0)
+    for p in range(2, LAST_PIECES):
+        start(("z", 2, 3, p))
+    landed(2, 1)
+    reduce(1)
+    for p in range(1, LAST_PIECES):
+        forward_z(2, 3, p)
+    pass_on(0)
+    for p in range(LAST_PIECES):
+        forward_y(2, 3, p)
     landed(2, 3)
-    reduce(3)
+    reduce(3, (1,))
+    start(("ox", 1, 1))
+    reduce(3, (0,))
+    start(("ox", 1, 0))
+    arrived(("ox", 0, 0), ("oz", 0))
+    pass_on(1)
+    arrived(("ox", 1, 0))
+    finish(1)
+    arrived(("oz", 1))
+    finish(0)
     for copy in copies.values():
         copy.wait_send()
 
 
 def fused(tokens, ln_gain, w_qkv, w_up, q_gain, k_gain, w_proj, w_down):
-    side = lax.axis_index("mp")
-    me = lax.axis_index("fsdp")
-    z = me // 4
-    half = z % 2
     rows, cols = tokens.shape
     depth = w_up.shape[0]
     heads = q_gain.shape[0] // 2
     head_cols, hidden = heads * HD, w_up.shape[1] // 2
     tall, whole, joint = 2 * rows, 16 * depth, head_cols + hidden
-    qkv = w_qkv.reshape(depth, 3, 2, head_cols).transpose(2, 0, 1, 3)
-    qkv = qkv.reshape(2, depth, 3 * head_cols)
     outs = jnp.concatenate(
         [w_proj.reshape(2, head_cols, depth), w_down.reshape(2, hidden, depth)], axis=1
     ).transpose(0, 2, 1)
     bf16, f32 = jnp.bfloat16, jnp.float32
     anywhere, vmem = pl.BlockSpec(memory_space=pl.ANY), pl.BlockSpec(memory_space=pltpu.VMEM)
-    terms = pl.pallas_call(
+    return pl.pallas_call(
         fused_kernel,
         out_shape=[
-            jax.ShapeDtypeStruct((4, tall, 4 * depth), bf16),
+            jax.ShapeDtypeStruct((rows, cols), bf16),
             jax.ShapeDtypeStruct((whole, 3 * head_cols), bf16),
             jax.ShapeDtypeStruct((whole, hidden), bf16),
             jax.ShapeDtypeStruct((whole, joint), bf16),
         ],
-        in_specs=[anywhere, vmem, vmem, vmem, anywhere, anywhere, anywhere],
+        in_specs=[anywhere, vmem, vmem, vmem] + [anywhere] * 5,
         out_specs=[vmem, anywhere, anywhere, anywhere],
         scratch_shapes=[
             pltpu.VMEM((2, tall, cols), bf16),
@@ -373,34 +451,22 @@
             pltpu.VMEM((tall, joint), bf16),
             pltpu.VMEM((2, whole, 256), bf16),
             pltpu.VMEM((2, 256, joint), bf16),
-            pltpu.SemaphoreType.DMA((48,)),
-            pltpu.SemaphoreType.DMA((48,)),
-            pltpu.SemaphoreType.DMA((4,)),
+            pltpu.VMEM((4, tall, 4 * depth), bf16),
+            pltpu.VMEM((2, tall, 4 * depth), bf16),
+            pltpu.VMEM((2, rows, 4 * depth), bf16),
+            pltpu.VMEM((2, rows, 4 * depth), bf16),
+            pltpu.SemaphoreType.DMA((SEMAPHORES,)),
+            pltpu.SemaphoreType.DMA((SEMAPHORES,)),
+            pltpu.SemaphoreType.DMA((6,)),
             pltpu.SemaphoreType.DMA((2,)),
         ],
         compiler_params=pltpu.CompilerParams(
             collective_id=0, has_side_effects=True, vmem_limit_bytes=58 * 2**20
         ),
-    )(tokens, ln_gain[None], q_gain, k_gain, qkv, w_up, outs)[0]
-
-    def swap(value, mask, axis="fsdp"):
-        count = 16 if axis == "fsdp" else 2
-        return lax.ppermute(value, axis, [(i, i ^ mask) for i in range(count)])
-
-    keep_low = z // 2 == side
-    own, far = [], []
-    for stage in range(2):
-        low, high = terms[stage], terms[stage + 2]
-        keep = jnp.where(keep_low, low, high)
-        got = swap(jnp.where(keep_low, high, low), 1, "mp")
-        total = keep.astype(f32) + got.astype(f32)
-        own.append(total[:rows])
-        far.append(swap(total[rows:].astype(bf16), 4))
-    done = [own[s] + far[1 - s].astype(f32) for s in range(2)]
-    branches = jnp.where(
-        half == 0, jnp.concatenate(done, axis=1), jnp.concatenate(done[::-1], axis=1)
-    )
-    return (tokens.astype(f32) + branches).astype(bf16)
+    )(
+        tokens, ln_gain[None], q_gain, k_gain,
+        w_qkv[:, 0], w_qkv[:, 1], w_qkv[:, 2], w_up, outs,
+    )[0]
 
 
 def solution(mesh):

time: 511 us -> 418 us (0.82)
  waiting for transfers between devices: 98.9 us -> 0 us
  Pallas kernels: 361 us -> 404 us
  starting transfers between devices: 22.8 us -> 0 us
  local copies, waits for them, and re-layouts: 16.4 us -> 6.75 us
  other arithmetic: 10.8 us -> 1.83 us
    ppermute x4 -> x0, waiting for transfers between devices: 98.9 us -> none  [swap(): return lax.ppermute(value, axis, [(i, i ^ mask) for i in range(count)])]
    pallas_call x1, Pallas kernels: 361 us -> 404 us  [fused(): pl.pallas_call(fused_kernel, out_shape=[jax.ShapeDtypeStruct((rows, cols)...]
    ppermute x4 -> x0, starting transfers between devices: 22.8 us -> none  [swap(): return lax.ppermute(value, axis, [(i, i ^ mask) for i in range(count)])]
    reshape x3 -> x0, local copies, waits for them, and re-layouts: 11.4 us -> none  [the longest x2 7.81 us: fused(): qkv = w_qkv.reshape(depth, 3, 2, head_cols).transpose(2, 0, 1, 3)]
  transfers between devices with their start and end apart: 4 -> 0, of which waited for: 4 -> 0; matrix products, arithmetic and copies ran while one was open for 1% -> 0% of each run, Pallas kernels for 0% -> 0%
where the time goes in v3:
time: 418 us; the launch traced here: 413 us
  Pallas kernels  404 us (97%)
  local copies, waits for them, and re-layouts  6.75 us (2%)
    pallas_call x1, Pallas kernels, fused(): pl.pallas_call(fused_kernel, out_shape=[jax.ShapeDtypeStruct((rows, cols)...  404 us

profile of v3, /device:TPU:0, one launch (start us, length us, event | category | flops | bytes accessed | tf_op | source)
XLA Modules:
  0.0 413.0 jit_solution(8636927769544843313)
XLA Ops:
  0.0 0.0 copy-start
  0.0 1.3 copy.16
  1.3 2.7 slice_bitcast_fusion
  3.9 0.0 copy-done
  3.9 0.2 copy.15
  4.1 1.8 maximum_bitcast_fusion.outs_ref
  5.9 404.4 %shard_map.82 = (bf16[512,1536]{1,0:T(8,128)(2,1)}, bf16[3072,2304]{1,0:T(8,128)(2,1)}, bf16[3072,3072]{1,0:T(8,128)(2,1)}, bf16[3072,3840]{1,0:T(8,128)(2,1)}) custom-call(bf16[512,1536]{1,0:T(8,128)(2,1)} %tokens_ref.1, f32[1,3072]{1,0:T(1,128)} %bitcast.21, f32[12,128]{1,0:T(8,128)} %qgain_ref.1, f32[12,128]{1,0:T(8,128)} %kgain_ref.1, ...), custom_call_target="tpu_custom_call" | custom-call | tf_op jit(solution)/shard_map/pallas_call | solution.py:437
  410.4 2.7 copy.18
Async XLA Ops:
  0.0 3.9 copy-start

commit v4 on v3

--- a/solution.py
+++ b/solution.py
@@ -240,7 +240,8 @@
                 into = pl.ds(pl.multiple_of(head_cols + step * width, width), width)
                 joined[at, into] = active.astype(jnp.bfloat16)
 
-            by_rows(run, 512)
+            run(near)
+            run(far)
 
         stream(first, count, in_tile, lambda i: all_up.at[:, columns(i)], body)
 
@@ -293,7 +294,7 @@
         lax.fori_loop(0, rows // 128, step, 0)
 
     def attend(first, count):
-        def step(i, _):
+        def step(i):
             image, head = lax.div(i, heads), lax.rem(i, heads)
             at = pl.ds(pl.multiple_of(image * PATCHES, PATCHES), PATCHES)
 
@@ -314,9 +315,13 @@
                 probs.astype(jnp.bfloat16), values, preferred_element_type=jnp.float32
             )
             joined[at, pl.ds(pl.multiple_of(head * HD, HD), HD)] = mixed.astype(jnp.bfloat16)
+
+        def group(i, _):
+            for j in range(heads // 2):
+                step(first + i * (heads // 2) + j)
             return 0
 
-        lax.fori_loop(first, first + count, step, 0)
+        lax.fori_loop(0, count // (heads // 2), group, 0)
 
     def normalise():
         def run(at):
@@ -387,22 +392,24 @@
     forward_y(1, 3)
     for k in range(4):
         landed(1, k)
-    expand(0, up_steps // 2)
+    third = up_steps // 3
+    expand(0, third)
+    start(("z", 2, 3, 0))
+    forward_y(2, 1)
+    expand(third, third)
     forward_z(2, 2)
-    start(("z", 2, 3, 0), ("z", 2, 3, 1))
-    forward_y(2, 1)
-    expand(up_steps // 2, up_steps - up_steps // 2)
-    landed(2, 0)
-    reduce(0)
+    start(("z", 2, 3, 1))
+    expand(2 * third, up_steps - 2 * third)
+    forward_z(2, 3, 0)
+    for p in range(2, LAST_PIECES):
+        start(("z", 2, 3, p))
+    for k in (0, 1):
+        landed(2, k)
+        reduce(k)
     forward_y(2, 2)
     landed(2, 2)
     reduce(2)
     start(("ox", 0, 1), ("ox", 0, 0))
-    forward_z(2, 3, 0)
-    for p in range(2, LAST_PIECES):
-        start(("z", 2, 3, p))
-    landed(2, 1)
-    reduce(1)
     for p in range(1, LAST_PIECES):
         forward_z(2, 3, p)
     pass_on(0)

time: 418 us -> 418 us (level)
  no operation moved by 1% of the time
where the time goes in v4:
time: 418 us; the launch traced here: 416 us
  Pallas kernels  407 us (97%)
  local copies, waits for them, and re-layouts  6.75 us (2%)
    pallas_call x1, Pallas kernels, fused(): pl.pallas_call(fused_kernel, out_shape=[jax.ShapeDtypeStruct((rows, cols)...  407 us

profile of v4, /device:TPU:0, one launch (start us, length us, event | category | flops | bytes accessed | tf_op | source)
XLA Modules:
  0.0 416.1 jit_solution(17366341005626974606)
XLA Ops:
  0.0 0.0 copy-start
  0.0 1.3 copy.16
  1.3 2.7 slice_bitcast_fusion
  3.9 0.0 copy-done
  3.9 0.2 copy.15
  4.1 1.8 maximum_bitcast_fusion.outs_ref
  5.9 407.5 %shard_map.82 = (bf16[512,1536]{1,0:T(8,128)(2,1)}, bf16[3072,2304]{1,0:T(8,128)(2,1)}, bf16[3072,3072]{1,0:T(8,128)(2,1)}, bf16[3072,3840]{1,0:T(8,128)(2,1)}) custom-call(bf16[512,1536]{1,0:T(8,128)(2,1)} %tokens_ref.1, f32[1,3072]{1,0:T(1,128)} %bitcast.21, f32[12,128]{1,0:T(8,128)} %qgain_ref.1, f32[12,128]{1,0:T(8,128)} %kgain_ref.1, ...), custom_call_target="tpu_custom_call" | custom-call | tf_op jit(solution)/shard_map/pallas_call | solution.py:444
  413.4 2.7 copy.18
Async XLA Ops:
  0.0 3.9 copy-start

commit v5 on v4

--- a/solution.py
+++ b/solution.py
@@ -269,6 +269,7 @@
 
     def pass_on(s):
         arrived(("ox", s, 1))
+        start(("ox", s, 0))
 
         def step(i, _):
             begin = pl.multiple_of(i * 128, 128)
@@ -403,23 +404,26 @@
     forward_z(2, 3, 0)
     for p in range(2, LAST_PIECES):
         start(("z", 2, 3, p))
-    for k in (0, 1):
-        landed(2, k)
-        reduce(k)
+    landed(2, 0)
+    reduce(0)
     forward_y(2, 2)
     landed(2, 2)
     reduce(2)
-    start(("ox", 0, 1), ("ox", 0, 0))
-    for p in range(1, LAST_PIECES):
+    start(("ox", 0, 1))
+    landed(2, 1)
+    reduce(1)
+    last = LAST_PIECES - 1
+    for p in range(1, last):
         forward_z(2, 3, p)
+        forward_y(2, 3, p - 1)
+    forward_z(2, 3, last)
+    forward_y(2, 3, last - 1)
     pass_on(0)
-    for p in range(LAST_PIECES):
-        forward_y(2, 3, p)
+    forward_y(2, 3, last)
     landed(2, 3)
     reduce(3, (1,))
     start(("ox", 1, 1))
     reduce(3, (0,))
-    start(("ox", 1, 0))
     arrived(("ox", 0, 0), ("oz", 0))
     pass_on(1)
     arrived(("ox", 1, 0))

time: 418 us -> 414 us (level)
  no operation moved by 1% of the time
where the time goes in v5:
time: 414 us
  Pallas kernels  405 us (98%)
  local copies, waits for them, and re-layouts  6.75 us (2%)
    pallas_call x1, Pallas kernels, fused(): pl.pallas_call(fused_kernel, out_shape=[jax.ShapeDtypeStruct((rows, cols)...  405 us

profile of v5, /device:TPU:0, one launch (start us, length us, event | category | flops | bytes accessed | tf_op | source)
XLA Modules:
  0.0 413.6 jit_solution(12121584290605612046)
XLA Ops:
  0.0 0.0 copy-start
  0.0 1.3 copy.16
  1.3 2.7 slice_bitcast_fusion
  3.9 0.0 copy-done
  3.9 0.2 copy.15
  4.1 1.8 maximum_bitcast_fusion.outs_ref
  5.9 405.0 %shard_map.82 = (bf16[512,1536]{1,0:T(8,128)(2,1)}, bf16[3072,2304]{1,0:T(8,128)(2,1)}, bf16[3072,3072]{1,0:T(8,128)(2,1)}, bf16[3072,3840]{1,0:T(8,128)(2,1)}) custom-call(bf16[512,1536]{1,0:T(8,128)(2,1)} %tokens_ref.1, f32[1,3072]{1,0:T(1,128)} %bitcast.21, f32[12,128]{1,0:T(8,128)} %qgain_ref.1, f32[12,128]{1,0:T(8,128)} %kgain_ref.1, ...), custom_call_target="tpu_custom_call" | custom-call | tf_op jit(solution)/shard_map/pallas_call | solution.py:448
  411.0 2.7 copy.18
Async XLA Ops:
  0.0 3.9 copy-start
